TPU v7x, 512 devices: a whole 4x4x16 slice. The times are simulated.
512 devices in a mesh: row: 16 (over x, y), col: 32 (over z, core).
Axes of the slice: x: 4, y: 4, z: 16, core: 2. Of those that a mesh axis runs over, the one named last changes fastest.
Arguments:
- tokens: bfloat16 [512, 8192], P('col', 'row'), may hold values from -6 to 6
- out_grad: bfloat16 [512, 8192], P('col', 'row'), may hold values from -1.5 to 1.5
- w_gate: bfloat16 [8192, 26624], P('row', 'col'), may hold values from -0.0625 to 0.0625
- w_up: bfloat16 [8192, 26624], P('row', 'col'), may hold values from -0.0625 to 0.0625
- w_down: bfloat16 [26624, 8192], P('col', 'row'), may hold values from -0.0390625 to 0.0390625
Outputs:
- grad_input: bfloat16 [512, 8192], P('col', 'row')
- grad_gate_w: bfloat16 [8192, 26624], P('row', 'col')
- grad_up_w: bfloat16 [8192, 26624], P('row', 'col')
- grad_down_w: bfloat16 [26624, 8192], P('col', 'row')
All inputs are finite; a program needn't handle non-finite values.
Results may differ from a plain program's by a relative error of at most 0.0049.
Values may be sent and summed in bfloat16 or wider, within the bound.
No kernel may reach another device: no remote copies, remote signals or barrier semaphores. Data moves between devices by JAX's collectives and lax.ppermute only.
A program may use at most 64 MiB of HBM per device.

v0:
```python
import jax
import jax.numpy as jnp
from jax import lax
from jax.sharding import PartitionSpec as P


def swiglu_back(gate, up, back):
    sig = jax.nn.sigmoid(gate)
    active = gate * sig
    hidden = (active * up).astype(jnp.bfloat16)
    grad_gate = (back * up * sig * (1.0 + gate * (1.0 - sig))).astype(jnp.bfloat16)
    grad_up = (back * active).astype(jnp.bfloat16)
    return (hidden, grad_gate, grad_up)


def per_device(tokens, out_grad, w_gate, w_up, w_down):
    all_tokens, all_grads = (
        lax.all_gather(tokens, "col", axis=0, tiled=True),
        lax.all_gather(out_grad, "col", axis=0, tiled=True),
    )
    gate_part = jnp.dot(all_tokens, w_gate, preferred_element_type=jnp.float32)
    up_part = jnp.dot(all_tokens, w_up, preferred_element_type=jnp.float32)
    back_part = jnp.einsum("td,fd->tf", all_grads, w_down, preferred_element_type=jnp.float32)
    gate, up, back = lax.psum((gate_part, up_part, back_part), "row")
    hidden, grad_gate, grad_up = swiglu_back(gate, up, back)
    first = jnp.einsum("tf,df->td", grad_gate, w_gate, preferred_element_type=jnp.float32)
    second = jnp.einsum("tf,df->td", grad_up, w_up, preferred_element_type=jnp.float32)
    grad_input = lax.psum_scatter(first + second, "col", scatter_dimension=0, tiled=True).astype(
        jnp.bfloat16
    )
    grad_gate_w = jnp.einsum(
        "td,tf->df", all_tokens, grad_gate, preferred_element_type=jnp.float32
    ).astype(jnp.bfloat16)
    grad_up_w = jnp.einsum(
        "td,tf->df", all_tokens, grad_up, preferred_element_type=jnp.float32
    ).astype(jnp.bfloat16)
    grad_down_w = jnp.einsum(
        "tf,td->fd", hidden, all_grads, preferred_element_type=jnp.float32
    ).astype(jnp.bfloat16)
    return (grad_input, grad_gate_w, grad_up_w, grad_down_w)


def solution(mesh):
    placed = (P("col", "row"), P("col", "row"), P("row", "col"), P("row", "col"), P("col", "row"))
    return jax.shard_map(
        per_device,
        mesh=mesh,
        in_specs=placed,
        out_specs=(P("col", "row"), P("row", "col"), P("row", "col"), P("col", "row")),
        check_vma=False,
    )
```

profile of v0, /device:TPU:2, one launch (start us, length us, event | category | flops | bytes accessed | tf_op | source)
XLA Modules:
  0.0 342.6 jit_solution(1787090362124352602)
XLA Ops:
  7.2 0.0 copy-start
  7.2 0.0 all-reduce.3.cloned.1.call-start
  7.2 38.0 %all_gather.7 = bf16[512,512]{1,0:T(8,128)(2,1)S(1)} all-gather(bf16[16,512]{1,0:T(8,128)(2,1)} %param.5), channel_id=1, replica_groups=mesh['row'=16,'col'=32] {'col'}, dimensions={0}, use_global_device_ids=true | all-gather | bytes 540672 | tf_op jit(solution)/shard_map/all_gather | solution.py:18
  45.3 0.0 copy-start.1
  45.3 28.9 %all_gather.6 = bf16[512,512]{1,0:T(8,128)(2,1)S(1)} all-gather(bf16[16,512]{1,0:T(8,128)(2,1)} %param.6), channel_id=1, replica_groups=mesh['row'=16,'col'=32] {'col'}, dimensions={0}, use_global_device_ids=true | all-gather | bytes 540672 | tf_op jit(solution)/shard_map/all_gather | solution.py:19
  74.2 0.0 copy-done
  74.2 0.0 copy-start.2
  74.2 1.9 fusion.7
  76.1 0.0 copy-done.1
  76.1 0.0 copy-start.6
  76.1 1.9 fusion.6
  77.9 0.0 copy-done.2
  77.9 0.0 copy-done.6
  77.9 1.9 fusion.5
  79.8 0.0 all-reduce.3.cloned.1.call-update
  79.8 0.0 reduce-scatter.2.cloned.1.call-start
  79.9 139.5 %all-reduce.3.cloned.1.call-done = (f32[512,832]{0,1:T(8,128)}, f32[512,832]{0,1:T(8,128)}, f32[512,832]{0,1:T(8,128)}) async-done(((f32[512,832]{0,1:T(8,128)}, f32[512,832]{0,1:T(8,128)}, f32[512,832]{0,1:T(8,128)}), (f32[512,832]{0,1:T(8,128)}, f32[512,832]{0,1:T(8,128)}, f32[512,832]{0,1:T(8,128)})) %all-reduce.3.cloned.1.call-update) | async-done | bytes 5111824 | tf_op jit(solution)/shard_map/psum | solution.py:24
  219.4 3.5 %multiply_convert_fusion.1 = (bf16[512,832]{0,1:T(8,128)(2,1)S(1)}, bf16[512,832]{0,1:T(8,128)(2,1)S(1)}) fusion(f32[512,832]{0,1:T(8,128)} %get-tuple-element.5, f32[512,832]{0,1:T(8,128)} %get-tuple-element.4, f32[512,832]{0,1:T(8,128)} %get-tuple-element.6), kind=kLoop, calls=%fused_computation.1 | loop fusion | flops 5537792 | bytes 6815744 | tf_op jit(solution)/shard_map/convert_element_type | solution.py:12
  222.9 0.0 copy-start.7
  222.9 0.9 copy-done.7
  223.8 0.7 fusion.8
  224.5 1.7 convolution_add_fusion
  226.2 0.0 reduce-scatter.2.cloned.1.call-update
  226.2 0.0 copy-start.5
  226.2 1.5 fusion.2
  227.8 0.0 copy-start.3
  227.8 0.0 copy-start.4
  227.8 2.8 fusion.1
  230.6 0.0 copy-done.5
  230.6 0.0 copy-done.3
  230.6 0.0 copy-done.4
  230.6 1.5 convolution_convert_fusion
  232.1 102.3 %reduce-scatter.2.cloned.1.call-done = f32[16,512]{1,0:T(8,128)} async-done(((f32[512,512]{1,0:T(8,128)}), f32[16,512]{1,0:T(8,128)}) %reduce-scatter.2.cloned.1.call-update) | async-done | bytes 32784 | tf_op jit(solution)/shard_map/reduce_scatter | solution.py:28
  334.4 1.4 convert_element_type.29
Async XLA Ops:
  7.2 67.0 %copy-start = (bf16[512,832]{0,1:T(8,128)(2,1)S(1)}, bf16[512,832]{0,1:T(8,128)(2,1)}, u32[]{:S(2)}) copy-start(bf16[512,832]{0,1:T(8,128)(2,1)} %param.7) | copy-start | bytes 2555908
  7.2 212.2 %all-reduce.3.cloned.1.call-start = ((), (), s32[]{:S(2)}) async-start(), calls=%async_computation.2 | async-start | bytes 10223616 | tf_op jit(solution)/shard_map/psum | solution.py:24
  45.3 30.8 %copy-start.1 = (bf16[512,832]{0,1:T(8,128)(2,1)S(1)}, bf16[512,832]{0,1:T(8,128)(2,1)}, u32[]{:S(2)}) copy-start(bf16[512,832]{0,1:T(8,128)(2,1)} %param.8) | copy-start | bytes 2555908
  74.2 3.8 %copy-start.2 = (bf16[512,512]{1,0:T(8,128)(2,1)}, bf16[512,512]{1,0:T(8,128)(2,1)S(1)}, u32[]{:S(2)}) copy-start(bf16[512,512]{1,0:T(8,128)(2,1)S(1)} %all_gather.6) | copy-start | bytes 1572868
  76.1 1.9 copy-start.6
  79.8 254.6 %reduce-scatter.2.cloned.1.call-start = ((), (), s32[]{:S(2)}) async-start(), calls=%async_computation.1 | async-start | bytes 1081344 | tf_op jit(solution)/shard_map/reduce_scatter | solution.py:28
  222.9 0.9 copy-start.7
  226.2 4.3 %copy-start.5 = (f32[512,832]{0,1:T(8,128)S(1)}, f32[512,832]{0,1:T(8,128)}, u32[]{:S(2)}) copy-start(f32[512,832]{0,1:T(8,128)} %get-tuple-element.6) | copy-start | bytes 5111812
  227.8 2.8 copy-start.3
  227.8 2.8 copy-start.4
Sparse Core Ops, SparseCore 0:
  80.0 139.3 all-reduce.2
  226.4 108.0 reduce-scatter.1
where the time goes:
time: 343 us
  waiting for transfers between devices  242 us (71%)
  blocking collectives  66.9 us (20%)
  between operations  14.1 us (4%)
  matrix products  13.9 us (4%)
  other arithmetic  4.82 us (1%)
    psum x1, waiting for transfers between devices, per_device(): gate, up, back = lax.psum((gate_part, up_part, back_part), 'row')  140 us
    reduce_scatter x1, waiting for transfers between devices, per_device(): lax.psum_scatter(first + second, 'col', scatter_dimension=0, tiled=True)  102 us
    all_gather x1, blocking collectives, per_device(): lax.all_gather(tokens, 'col', axis=0, tiled=True)  38 us
    all_gather x1, blocking collectives, per_device(): lax.all_gather(out_grad, 'col', axis=0, tiled=True)  28.9 us
  transfers between devices with their start and end apart: 2, of which 2 were waited for; matrix products, arithmetic and copies ran while one was open for 2% of the time, Pallas kernels for 0%

commit v1 on v0

v1 whole, which is shorter than its diff:
```python
import jax
import jax.numpy as jnp
from jax import lax
from jax.sharding import Mesh, PartitionSpec as P

ROW = ("x", "y")
SWAP = [(0, 1), (1, 0)]


def swiglu_back(gate, up, back):
    sig = jax.nn.sigmoid(gate)
    active = gate * sig
    hidden = (active * up).astype(jnp.bfloat16)
    grad_gate = (back * up * sig * (1.0 + gate * (1.0 - sig))).astype(jnp.bfloat16)
    grad_up = (back * active).astype(jnp.bfloat16)
    return (hidden, grad_gate, grad_up)


def dot(spec, a, b):
    return jnp.einsum(spec, a, b, preferred_element_type=jnp.float32)


def per_device(tokens, out_grad, w_gate, w_up, w_down):
    own = lax.all_gather(jnp.concatenate([tokens, out_grad], 1), "z", axis=0, tiled=True)
    other = lax.ppermute(own, "c", SWAP)
    both = jnp.concatenate([own, other], 0)
    width, hid = w_gate.shape
    count = both.shape[0]
    all_tokens, all_grads = both[:, :width], both[:, width:]
    parts = jnp.concatenate(
        [
            dot("td,df->tf", all_tokens, w_gate).astype(jnp.bfloat16),
            dot("td,df->tf", all_tokens, w_up).astype(jnp.bfloat16),
            dot("td,fd->tf", all_grads, w_down).astype(jnp.bfloat16),
        ],
        1,
    )
    rows = lax.axis_size("x") * lax.axis_size("y")
    parts = parts.reshape(rows, count // rows, 3 * hid)
    parts = lax.all_to_all(parts, ROW, split_axis=0, concat_axis=0, tiled=True)
    total = jnp.sum(parts.astype(jnp.float32), 0)
    made = swiglu_back(total[:, :hid], total[:, hid : 2 * hid], total[:, 2 * hid :])
    made = jnp.concatenate(made, 1)
    made = jnp.broadcast_to(made[None], (rows,) + made.shape)
    made = lax.all_to_all(made, ROW, split_axis=0, concat_axis=0, tiled=True)
    made = made.reshape(count, 3 * hid)
    hidden, grad_gate, grad_up = made[:, :hid], made[:, hid : 2 * hid], made[:, 2 * hid :]
    part = dot("tf,df->td", grad_gate, w_gate) + dot("tf,df->td", grad_up, w_up)
    part = part[: count // 2] + lax.ppermute(part[count // 2 :], "c", SWAP)
    depth = lax.axis_size("z")
    part = part.astype(jnp.bfloat16).reshape(depth, count // 2 // depth, width)
    part = lax.all_to_all(part, "z", split_axis=0, concat_axis=0, tiled=True)
    grad_input = jnp.sum(part.astype(jnp.float32), 0).astype(jnp.bfloat16)
    grad_gate_w = dot("td,tf->df", all_tokens, grad_gate).astype(jnp.bfloat16)
    grad_up_w = dot("td,tf->df", all_tokens, grad_up).astype(jnp.bfloat16)
    grad_down_w = dot("tf,td->fd", hidden, all_grads).astype(jnp.bfloat16)
    return (grad_input, grad_gate_w, grad_up_w, grad_down_w)


def solution(mesh):
    mesh = Mesh(mesh.devices.reshape(4, 4, 16, 2), ("x", "y", "z", "c"))
    col = ("z", "c")
    placed = (P(col, ROW), P(col, ROW), P(ROW, col), P(ROW, col), P(col, ROW))
    return jax.shard_map(
        per_device,
        mesh=mesh,
        in_specs=placed,
        out_specs=(P(col, ROW), P(ROW, col), P(ROW, col), P(col, ROW)),
        check_vma=False,
    )
```

time: 343 us -> 162 us (0.47)
  the two profiles are of different devices: /device:TPU:2 before, /device:TPU:32 now
where the time goes in v1:
time: 162 us
  blocking collectives  114 us (70%)
  waiting for transfers between devices  15.9 us (10%)
  starting transfers between devices  12.7 us (8%)
  matrix products  9.6 us (6%)
  other arithmetic  5.41 us (3%)
  local copies, waits for them, and re-layouts  3.85 us (2%)
    all_to_all x1, blocking collectives, per_device(): parts = lax.all_to_all(parts, ROW, split_axis=0, concat_axis=0, tiled=True)  41.1 us
    all_to_all x1, blocking collectives, per_device(): made = lax.all_to_all(made, ROW, split_axis=0, concat_axis=0, tiled=True)  36.4 us
    all_gather x1, blocking collectives, per_device(): lax.all_gather(jnp.concatenate([tokens, out_grad], 1), 'z', axis=0, tiled...  36.1 us
    all_to_all x1, waiting for transfers between devices, per_device(): part = lax.all_to_all(part, 'z', split_axis=0, concat_axis=0, tiled=True)  12.2 us
    dot_general x8, matrix products, dot(): return jnp.einsum(spec, a, b, preferred_element_type=jnp.float32)  9.6 us
    all_to_all x1, starting transfers between devices, per_device(): part = lax.all_to_all(part, 'z', split_axis=0, concat_axis=0, tiled=True)  8.87 us
  transfers between devices with their start and end apart: 3, of which 3 were waited for; matrix products, arithmetic and copies ran while one was open for 4% of the time, Pallas kernels for 0%

profile of v1, /device:TPU:32, one launch (start us, length us, event | category | flops | bytes accessed | tf_op | source)
XLA Modules:
  0.0 161.8 jit_solution(6133314187838807101)
XLA Ops:
  0.6 0.0 copy-start
  0.6 0.0 copy-start.1
  0.7 0.0 copy-start.5
  0.7 0.9 pad_maximum_fusion.1
  1.6 36.1 %all_gather.3 = bf16[256,1024]{1,0:T(8,128)(2,1)S(1)} all-gather(bf16[16,1024]{1,0:T(8,128)(2,1)S(1)} %pad_maximum_fusion.1), channel_id=1, replica_groups=mesh['x'=4,'y'=4,'z'=16,'c'=2] {'z'}, dimensions={0}, use_global_device_ids=true | all-gather | bytes 557056 | tf_op jit(solution)/shard_map/all_gather | solution.py:24
  37.6 1.9 %collective-permute-start = (bf16[256,1024]{1,0:T(8,128)(2,1)S(1)}, bf16[256,1024]{1,0:T(8,128)(2,1)S(1)}, u32[]{:S(2)}, u32[]{:S(2)}) collective-permute-start(bf16[256,1024]{1,0:T(8,128)(2,1)S(1)} %all_gather.3), channel_id=1, source_target_pairs={{0,1},{1,0},{2,3},{3,2},{4,5},{5,4},{6,7},{7,6},{8,9},{9,8},{10,11... | collective-permute-start | bytes 1572872 | tf_op jit(solution)/shard_map/ppermute | solution.py:25
  39.6 1.8 %collective-permute-done = bf16[256,1024]{1,0:T(8,128)(2,1)S(1)} collective-permute-done((bf16[256,1024]{1,0:T(8,128)(2,1)S(1)}, bf16[256,1024]{1,0:T(8,128)(2,1)S(1)}, u32[]{:S(2)}, u32[]{:S(2)}) %collective-permute-start) | collective-permute-done | bytes 524320 | tf_op jit(solution)/shard_map/ppermute | solution.py:25
  41.5 0.0 copy-done.1
  41.5 0.0 copy-start.3
  41.5 0.6 convolution_convert_fusion.4
  42.1 0.0 copy-done.5
  42.1 0.6 convolution_convert_fusion.3
  42.8 0.0 copy-done.3
  42.8 0.0 copy-done
  42.8 0.6 convolution_convert_fusion.5
  43.4 1.7 %pad_maximum_fusion = bf16[512,2496]{0,1:T(8,128)(2,1)} fusion(bf16[512,832]{0,1:T(8,128)(2,1)S(1)} %convolution_convert_fusion.3, bf16[512,832]{0,1:T(8,128)(2,1)S(1)} %convolution_convert_fusion.4, bf16[512,832]{0,1:T(8,128)(2,1)S(1)} %convolution_convert_fusion.5), kind=kLoop, calls=%fused_computation.1 | loop fusion | flops 7667712 | bytes 5111808 | tf_op jit(solution)/shard_map/concatenate | solution.py:30
  45.1 3.0 %copy.9 = bf16[512,2496]{1,0:T(8,128)(2,1)S(1)} copy(bf16[512,2496]{0,1:T(8,128)(2,1)} %pad_maximum_fusion) | data formatting | bytes 5111808 | tf_op jit(solution)/shard_map/concatenate | solution.py:30
  48.1 41.1 %all_to_all.15 = bf16[16,32,2496]{2,1,0:T(8,128)(2,1)S(1)} all-to-all(bf16[16,32,2496]{2,1,0:T(8,128)(2,1)S(1)} %bitcast.8), channel_id=1, replica_groups=mesh['x'=4,'y'=4,'z'=16,'c'=2] {'x','y'}, dimensions={0} | all-to-all | bytes 5111808 | tf_op jit(solution)/shard_map/all_to_all | solution.py:40
  89.2 0.4 convert_reduce_fusion
  89.5 0.1 multiply_convert_fusion
  89.7 0.1 concatenate.15
  89.8 0.2 broadcast_in_dim.2
  90.0 36.4 %all_to_all.16 = bf16[16,32,2496]{2,1,0:T(8,128)(2,1)S(1)} all-to-all(bf16[16,32,2496]{2,1,0:T(8,128)(2,1)S(1)} %broadcast_in_dim.2), channel_id=1, replica_groups=mesh['x'=4,'y'=4,'z'=16,'c'=2] {'x','y'}, dimensions={0} | all-to-all | bytes 5111808 | tf_op jit(solution)/shard_map/all_to_all | solution.py:45
  126.4 0.0 copy-start.2
  126.4 0.8 fusion.4
  127.1 0.4 copy-done.2
  127.5 0.7 convolution_add_fusion
  128.3 1.9 %collective-permute-start.1 = (f32[256,512]{1,0:T(8,128)S(1)}, f32[256,512]{1,0:T(8,128)S(1)}, u32[]{:S(2)}, u32[]{:S(2)}) collective-permute-start(f32[256,512]{1,0:T(8,128)S(1)} %slice.48), channel_id=1, source_target_pairs={{0,1},{1,0},{2,3},{3,2},{4,5},{5,4},{6,7},{7,6},{8,9},{9,8},{10,11... | collective-permute-start | bytes 1572872 | tf_op jit(solution)/shard_map/ppermute | solution.py:49
  130.2 1.9 %collective-permute-done.1 = f32[256,512]{1,0:T(8,128)S(1)} collective-permute-done((f32[256,512]{1,0:T(8,128)S(1)}, f32[256,512]{1,0:T(8,128)S(1)}, u32[]{:S(2)}, u32[]{:S(2)}) %collective-permute-start.1) | collective-permute-done | bytes 524320 | tf_op jit(solution)/shard_map/ppermute | solution.py:49
  132.1 0.8 fusion.6
  132.9 8.9 %all-to-all-start.2 = ((bf16[16,16,512]{2,1,0:T(8,128)(2,1)}), bf16[16,16,512]{2,1,0:T(8,128)(2,1)}, u32[]{:S(2)}, u32[]{:S(2)}) async-start(bf16[16,16,512]{2,1,0:T(8,128)(2,1)} %bitcast.14), calls=%async_computation.2 | async-start | bytes 524288 | tf_op jit(solution)/shard_map/all_to_all | solution.py:52
  141.7 0.0 copy-start.4
  141.7 3.1 %convolution_convert_fusion.2 = bf16[512,832]{0,1:T(8,128)(2,1)} fusion(bf16[512,2496]{1,0:T(8,128)(2,1)S(1)} %bitcast.11, bf16[512,1024]{1,0:T(8,128)(2,1)} %copy-done.3), kind=kOutput, calls=%fused_computation.4 | convolution fusion | flops 436633600 | bytes 2293760 | tf_op jit(solution)/shard_map/td,tf->df/dot_general | solution.py:20
  144.9 0.0 copy-done.4
  144.9 1.6 convolution_convert_fusion.1
  146.4 1.5 convolution_convert_fusion
  148.0 12.2 %all-to-all-done.2 = bf16[16,16,512]{2,1,0:T(8,128)(2,1)} async-done(((bf16[16,16,512]{2,1,0:T(8,128)(2,1)}), bf16[16,16,512]{2,1,0:T(8,128)(2,1)}, u32[]{:S(2)}, u32[]{:S(2)}) %all-to-all-start.2) | async-done | bytes 262176 | tf_op jit(solution)/shard_map/all_to_all | solution.py:52
  160.2 1.6 reduce_sum.22
  (3 shorter events, 0.1 us)
Async XLA Ops:
  0.6 42.2 %copy-start = (bf16[512,832]{0,1:T(8,128)(2,1)S(1)}, bf16[512,832]{0,1:T(8,128)(2,1)}, u32[]{:S(2)}) copy-start(bf16[512,832]{0,1:T(8,128)(2,1)} %param.7) | copy-start | bytes 2555908
  0.6 40.8 %copy-start.1 = (bf16[512,832]{0,1:T(8,128)(2,1)S(1)}, bf16[512,832]{0,1:T(8,128)(2,1)}, u32[]{:S(2)}) copy-start(bf16[512,832]{0,1:T(8,128)(2,1)} %param.8) | copy-start | bytes 2555908
  0.7 41.5 %copy-start.5 = (bf16[832,512]{1,0:T(8,128)(2,1)S(1)}, bf16[832,512]{1,0:T(8,128)(2,1)}, u32[]{:S(2)}) copy-start(bf16[832,512]{1,0:T(8,128)(2,1)} %param.9) | copy-start | bytes 2555908
  37.6 3.8 %collective-permute-start = (bf16[256,1024]{1,0:T(8,128)(2,1)S(1)}, bf16[256,1024]{1,0:T(8,128)(2,1)S(1)}, u32[]{:S(2)}, u32[]{:S(2)}) collective-permute-start(bf16[256,1024]{1,0:T(8,128)(2,1)S(1)} %all_gather.3), channel_id=1, source_target_pairs={{0,1},{1,0},{2,3},{3,2},{4,5},{5,4},{6,7},{7,6},{8,9},{9,8},{10,11... | collective-permute-start | bytes 1572872 | tf_op jit(solution)/shard_map/ppermute | solution.py:25
  41.5 1.3 copy-start.3
  126.4 1.2 copy-start.2
  128.3 3.8 %collective-permute-start.1 = (f32[256,512]{1,0:T(8,128)S(1)}, f32[256,512]{1,0:T(8,128)S(1)}, u32[]{:S(2)}, u32[]{:S(2)}) collective-permute-start(f32[256,512]{1,0:T(8,128)S(1)} %slice.48), channel_id=1, source_target_pairs={{0,1},{1,0},{2,3},{3,2},{4,5},{5,4},{6,7},{7,6},{8,9},{9,8},{10,11... | collective-permute-start | bytes 1572872 | tf_op jit(solution)/shard_map/ppermute | solution.py:49
  132.9 27.3 %all-to-all-start.2 = ((bf16[16,16,512]{2,1,0:T(8,128)(2,1)}), bf16[16,16,512]{2,1,0:T(8,128)(2,1)}, u32[]{:S(2)}, u32[]{:S(2)}) async-start(bf16[16,16,512]{2,1,0:T(8,128)(2,1)} %bitcast.14), calls=%async_computation.2 | async-start | bytes 524288 | tf_op jit(solution)/shard_map/all_to_all | solution.py:52
  141.7 3.1 %copy-start.4 = (bf16[512,1024]{1,0:T(8,128)(2,1)S(1)}, bf16[512,1024]{1,0:T(8,128)(2,1)}, u32[]{:S(2)}) copy-start(bf16[512,1024]{1,0:T(8,128)(2,1)} %copy-done.3) | copy-start | bytes 3145732

commit v2 on v0

v2 whole, which is shorter than its diff:
```python
import functools


import jax
import jax.numpy as jnp
from jax import lax
from jax.experimental import pallas as pl
from jax.experimental.pallas import tpu as pltpu
from jax.sharding import Mesh, PartitionSpec as P

ROW = ("x", "y")
SWAP = [(0, 1), (1, 0)]
B, F = jnp.bfloat16, jnp.float32
SIDE = 4
NN, NT, TN = ((1,), (0,)), ((1,), (1,)), ((0,), (0,))


def call(body, outs, *args, weights=(), scratch=()):
    many = isinstance(outs, list)
    shapes = [jax.ShapeDtypeStruct(s, d) for s, d in (outs if many else [outs])]
    made = pl.pallas_call(
        body,
        out_shape=shapes,
        in_specs=[pl.BlockSpec(memory_space=pltpu.HBM)] * len(weights)
        + [pl.BlockSpec(memory_space=pltpu.VMEM)] * len(args),
        out_specs=[pl.BlockSpec(memory_space=pltpu.VMEM)] * len(shapes),
        scratch_shapes=list(scratch),
        compiler_params=pltpu.CompilerParams(vmem_limit_bytes=24 << 20),
        cost_estimate=pl.CostEstimate(flops=1 << 30, bytes_accessed=4 << 20, transcendentals=0),
    )(*weights, *args)
    return made if many else made[0]


def mm(a, b, dims):
    return lax.dot_general(a, b, (dims, ((), ())), preferred_element_type=F)


def products(weights, tokens, store):
    hid, width = weights[0].shape
    rows, lanes = hid // SIDE, 2 * tokens.shape[0] // SIDE
    for i, w in enumerate(weights):
        part = mm(w[...], tokens[:, width:] if i == 2 else tokens[:, :width], NT).astype(B)
        for k in range(SIDE // 2):
            for j in range(SIDE):
                store(k, j, i, part[j * rows : (j + 1) * rows, k * lanes : (k + 1) * lanes])


def own_parts_kernel(wg, wu, wd, own, out, *held_and_sems):
    *held, sems = held_and_sems
    copies = [pltpu.make_async_copy(w, v, sems.at[i]) for i, (w, v) in enumerate(zip((wg, wu, wd), held))]
    for copy in copies:
        copy.start()
    for copy in copies:
        copy.wait()

    def store(k, j, i, part):
        out[k * SIDE + j, i] = part

    products(held, own, store)


def parts_kernel(other, first, wg, wu, wd, out):
    half = first.shape[0]

    def store(k, j, i, part):
        out[half + k * SIDE + j, i] = part
        out[k * SIDE + j, i] = first[k * SIDE + j, i]

    products((wg, wu, wd), other, store)


def back_kernel(got, spread, hidden):
    gate, up, back = (sum(got[r, i].astype(F) for r in range(got.shape[0])) for i in range(3))
    sig = jax.nn.sigmoid(gate)
    active = gate * sig
    hidden[...] = (active * up).astype(B)
    grad_gate = (back * up * sig * (1.0 + gate * (1.0 - sig))).astype(B)
    grad_up = (back * active).astype(B)
    for r in range(spread.shape[0]):
        spread[r, 0] = grad_gate
        spread[r, 1] = grad_up


def all_of(blocks, half=None):
    chosen = range(SIDE) if half is None else range(half * SIDE // 2, (half + 1) * SIDE // 2)
    columns = [jnp.concatenate([blocks(i, j) for j in range(SIDE)], 0) for i in chosen]
    return jnp.concatenate(columns, 1)


def input_kernel(half, grads, wg, wu, out):
    out[...] = sum(
        mm(all_of(lambda i, j: grads[i * SIDE + j, p], half), w[...], TN) for p, w in enumerate((wg, wu))
    )


def gate_up_kernel(grads, own, other, *outs):
    half, width = own.shape[0], outs[0].shape[1]
    for p, out in enumerate(outs):
        g = all_of(lambda i, j: grads[i * SIDE + j, p])
        part = mm(g[:, :half], own[:, :width], NN) + mm(g[:, half:], other[:, :width], NN)
        out[...] = part.astype(B)


def down_kernel(hidden, own, other, out):
    half, width = own.shape[0], out.shape[1]
    h = all_of(lambda i, j: hidden[i * SIDE + j])
    part = mm(h[:, :half], own[:, width:], NN) + mm(h[:, half:], other[:, width:], NN)
    out[...] = part.astype(B)


def spread_over(x, axes):
    return lax.all_to_all(x, axes, split_axis=0, concat_axis=0, tiled=True)


def per_device(tokens, out_grad, w_gate, w_up, w_down):
    hid, width = w_down.shape
    depth = lax.axis_size("z")
    own = lax.all_gather(jnp.concatenate([tokens, out_grad], 1), "z", axis=0, tiled=True)
    other = lax.ppermute(own, "c", SWAP)
    half = own.shape[0]
    rows, lanes, ranks = hid // SIDE, 2 * half // SIDE, SIDE * SIDE
    wg, wu, w_down = (pltpu.with_memory_space_constraint(w, pltpu.HBM) for w in (w_gate.T, w_up.T, w_down))

    sizes = (ranks, 3, rows, lanes)
    parts, *held = call(
        own_parts_kernel,
        [((ranks // 2,) + sizes[1:], B)] + [((hid, width), B)] * 3,
        own,
        weights=(wg, wu, w_down),
        scratch=[pltpu.SemaphoreType.DMA((3,))],
    )
    parts = call(parts_kernel, (sizes, B), other, parts, *held)
    spread, hidden = call(
        back_kernel, [((ranks, 2, rows, lanes), B), ((rows, lanes), B)], spread_over(parts, ROW)
    )
    grads = spread_over(spread, ROW)
    hidden = lax.all_gather(hidden, ROW, axis=0, tiled=False)

    rest, mine = (
        call(functools.partial(input_kernel, h), ((half, width), F), grads, *held[:2]) for h in (1, 0)
    )
    part = (mine + lax.ppermute(rest, "c", SWAP)).astype(B)
    part = spread_over(part.reshape(depth, half // depth, width), "z")
    grad_input = jnp.sum(part.astype(F), 0).astype(B)
    grad_gate_w, grad_up_w = call(gate_up_kernel, [((hid, width), B)] * 2, grads, own, other)
    grad_down_w = call(down_kernel, ((hid, width), B), hidden, own, other)
    return (grad_input, grad_gate_w.T, grad_up_w.T, grad_down_w)


def solution(mesh):
    shape = (SIDE, SIDE, mesh.devices.shape[1] // 2, 2)
    mesh = Mesh(mesh.devices.reshape(shape), ("x", "y", "z", "c"))
    col = ("z", "c")
    placed = (P(col, ROW), P(col, ROW), P(ROW, col), P(ROW, col), P(col, ROW))
    return jax.shard_map(
        per_device,
        mesh=mesh,
        in_specs=placed,
        out_specs=(P(col, ROW), P(ROW, col), P(ROW, col), P(col, ROW)),
        check_vma=False,
    )
```

time: 343 us -> 153 us (0.45)
  the two profiles are of different devices: /device:TPU:2 before, /device:TPU:32 now
where the time goes in v2:
time: 153 us; the launch traced here: 152 us
  blocking collectives  127 us (83%)
  starting transfers between devices  12.7 us (8%)
  Pallas kernels  8.92 us (6%)
  other arithmetic  2.15 us (1%)
    all_to_all x2, blocking collectives, spread_over(): return lax.all_to_all(x, axes, split_axis=0, concat_axis=0, tiled=True)  67.6 us
    all_gather x1, blocking collectives, per_device(): lax.all_gather(jnp.concatenate([tokens, out_grad], 1), 'z', axis=0, tiled...  36.1 us
    all_gather x1, blocking collectives, per_device(): hidden = lax.all_gather(hidden, ROW, axis=0, tiled=False)  23.1 us
    pallas_call x7, Pallas kernels, call(): pl.pallas_call(body, out_shape=shapes, in_specs=[pl.BlockSpec(memory_spac...  8.92 us
    all_to_all x1, starting transfers between devices, spread_over(): return lax.all_to_all(x, axes, split_axis=0, concat_axis=0, tiled=True)  8.85 us
  transfers between devices with their start and end apart: 3, of which 1 were waited for; matrix products, arithmetic and copies ran while one was open for 0% of the time, Pallas kernels for 5%

profile of v2, /device:TPU:32, one launch (start us, length us, event | category | flops | bytes accessed | tf_op | source)
XLA Modules:
  0.0 152.3 jit_solution(157507671690630610)
XLA Ops:
  0.6 0.7 pad_maximum_fusion
  1.4 36.1 %all_gather.9.own = bf16[256,1024]{1,0:T(8,128)(2,1)S(1)} all-gather(bf16[16,1024]{1,0:T(8,128)(2,1)S(1)} %pad_maximum_fusion), channel_id=1, replica_groups=mesh['x'=4,'y'=4,'z'=16,'c'=2] {'z'}, dimensions={0}, use_global_device_ids=true | all-gather | bytes 557056 | tf_op jit(solution)/shard_map/all_gather | solution.py:118
  37.4 1.9 %collective-permute-start = (bf16[256,1024]{1,0:T(8,128)(2,1)S(1)}, bf16[256,1024]{1,0:T(8,128)(2,1)S(1)}, u32[]{:S(2)}, u32[]{:S(2)}) collective-permute-start(bf16[256,1024]{1,0:T(8,128)(2,1)S(1)} %all_gather.9.own), channel_id=1, source_target_pairs={{0,1},{1,0},{2,3},{3,2},{4,5},{5,4},{6,7},{7,6},{8,9},{9,8},{10,11... | collective-permute-start | bytes 1572872 | tf_op jit(solution)/shard_map/ppermute | solution.py:119
  39.4 2.6 %shard_map.84 = (bf16[8,3,208,128]{3,2,1,0:T(8,128)(2,1)S(1)}, bf16[832,512]{1,0:T(8,128)(2,1)S(1)}, bf16[832,512]{1,0:T(8,128)(2,1)S(1)}, bf16[832,512]{1,0:T(8,128)(2,1)S(1)}) custom-call(bf16[832,512]{1,0:T(8,128)(2,1)} %bitcast.7, bf16[832,512]{1,0:T(8,128)(2,1)} %bitcast.8, bf16[832,512]{1,0:T(8,128)(2,1)} %wd.1, bf16[256,1024]{1,0:T(8,128)(2,1)S(1)} %all_gather.9.own), custom_call_target="tpu_custom_call" | custom-call | flops 1073741824 | bytes 4194304 | tf_op jit(solution)/shard_map/pallas_call | solution.py:21
  41.9 0.0 collective-permute-done.other
  41.9 1.0 shard_map.85
  42.9 40.8 %all_to_all.15.got = bf16[16,3,208,128]{3,2,1,0:T(8,128)(2,1)S(1)} all-to-all(bf16[16,3,208,128]{3,2,1,0:T(8,128)(2,1)S(1)} %shard_map.85), channel_id=1, replica_groups=mesh['x'=4,'y'=4,'z'=16,'c'=2] {'x','y'}, dimensions={0} | all-to-all | bytes 5111808 | tf_op jit(solution)/shard_map/all_to_all | solution.py:112
  83.6 0.4 shard_map.86
  84.0 26.8 %all_to_all.16.grads = bf16[16,2,208,128]{3,2,1,0:T(8,128)(2,1)S(1)} all-to-all(bf16[16,2,208,128]{3,2,1,0:T(8,128)(2,1)S(1)} %get-tuple-element.16), channel_id=1, replica_groups=mesh['x'=4,'y'=4,'z'=16,'c'=2] {'x','y'}, dimensions={0} | all-to-all | bytes 3407872 | tf_op jit(solution)/shard_map/all_to_all | solution.py:112
  110.8 0.7 shard_map.88
  111.5 1.9 %collective-permute-start.1 = (f32[256,512]{1,0:T(8,128)S(1)}, f32[256,512]{1,0:T(8,128)S(1)}, u32[]{:S(2)}, u32[]{:S(2)}) collective-permute-start(f32[256,512]{1,0:T(8,128)S(1)} %shard_map.88), channel_id=1, source_target_pairs={{0,1},{1,0},{2,3},{3,2},{4,5},{5,4},{6,7},{7,6},{8,9},{9,8},{10,11... | collective-permute-start | bytes 1572872 | tf_op jit(solution)/shard_map/ppermute | solution.py:142
  113.5 0.7 shard_map.87
  114.2 1.1 collective-permute-done.1
  115.4 0.8 add_convert_fusion
  116.1 8.9 %all-to-all-start.2 = ((bf16[16,16,512]{2,1,0:T(8,128)(2,1)}), bf16[16,16,512]{2,1,0:T(8,128)(2,1)S(1)}, u32[]{:S(2)}, u32[]{:S(2)}) async-start(bf16[16,16,512]{2,1,0:T(8,128)(2,1)} %bitcast.2), calls=%async_computation.2 | async-start | bytes 524288 | tf_op jit(solution)/shard_map/all_to_all | solution.py:112
  125.0 23.1 %all-gather = bf16[3328,128]{1,0:T(8,128)(2,1)S(1)} all-gather(bf16[208,128]{1,0:T(8,128)(2,1)S(1)} %get-tuple-element.19), channel_id=2, replica_groups=mesh['x'=4,'y'=4,'z'=16,'c'=2] {'x','y'}, dimensions={0}, use_global_device_ids=true | all-gather | bytes 905216 | tf_op jit(solution)/shard_map/all_gather | solution.py:137
  148.0 1.5 shard_map.90
  149.5 2.1 %shard_map.89 = (bf16[832,512]{1,0:T(8,128)(2,1)}, bf16[832,512]{1,0:T(8,128)(2,1)}) custom-call(bf16[16,2,208,128]{3,2,1,0:T(8,128)(2,1)S(1)} %all_to_all.16.grads, bf16[256,1024]{1,0:T(8,128)(2,1)S(1)} %all_gather.9.own, bf16[256,1024]{1,0:T(8,128)(2,1)S(1)} %collective-permute-done.other), custom_call_target="tpu_custom_call" | custom-call | flops 1073741824 | bytes 4194304 | tf_op jit(solution)/shard_map/pallas_call | solution.py:21
  151.6 0.0 all-to-all-done.2
  151.6 0.6 reduce_sum.12
Async XLA Ops:
  37.4 4.5 %collective-permute-start = (bf16[256,1024]{1,0:T(8,128)(2,1)S(1)}, bf16[256,1024]{1,0:T(8,128)(2,1)S(1)}, u32[]{:S(2)}, u32[]{:S(2)}) collective-permute-start(bf16[256,1024]{1,0:T(8,128)(2,1)S(1)} %all_gather.9.own), channel_id=1, source_target_pairs={{0,1},{1,0},{2,3},{3,2},{4,5},{5,4},{6,7},{7,6},{8,9},{9,8},{10,11... | collective-permute-start | bytes 1572872 | tf_op jit(solution)/shard_map/ppermute | solution.py:119
  111.5 3.8 %collective-permute-start.1 = (f32[256,512]{1,0:T(8,128)S(1)}, f32[256,512]{1,0:T(8,128)S(1)}, u32[]{:S(2)}, u32[]{:S(2)}) collective-permute-start(f32[256,512]{1,0:T(8,128)S(1)} %shard_map.88), channel_id=1, source_target_pairs={{0,1},{1,0},{2,3},{3,2},{4,5},{5,4},{6,7},{7,6},{8,9},{9,8},{10,11... | collective-permute-start | bytes 1572872 | tf_op jit(solution)/shard_map/ppermute | solution.py:142
  116.1 35.5 %all-to-all-start.2 = ((bf16[16,16,512]{2,1,0:T(8,128)(2,1)}), bf16[16,16,512]{2,1,0:T(8,128)(2,1)S(1)}, u32[]{:S(2)}, u32[]{:S(2)}) async-start(bf16[16,16,512]{2,1,0:T(8,128)(2,1)} %bitcast.2), calls=%async_computation.2 | async-start | bytes 524288 | tf_op jit(solution)/shard_map/all_to_all | solution.py:112

commit v3 on v2

--- a/solution.py
+++ b/solution.py
@@ -22,7 +22,7 @@
         body,
         out_shape=shapes,
         in_specs=[pl.BlockSpec(memory_space=pltpu.HBM)] * len(weights)
-        + [pl.BlockSpec(memory_space=pltpu.VMEM)] * len(args),
+        + [pl.BlockSpec(memory_space=pltpu.SMEM if a.dtype == jnp.int32 else pltpu.VMEM) for a in args],
         out_specs=[pl.BlockSpec(memory_space=pltpu.VMEM)] * len(shapes),
         scratch_shapes=list(scratch),
         compiler_params=pltpu.CompilerParams(vmem_limit_bytes=24 << 20),
@@ -101,11 +101,14 @@
         out[...] = part.astype(B)
 
 
-def down_kernel(hidden, own, other, out):
+def down_kernel(hidden, own, other, y, out):
     half, width = own.shape[0], out.shape[1]
-    h = all_of(lambda i, j: hidden[i * SIDE + j])
+    rows = out.shape[0] // SIDE
+    h = all_of(lambda i, k: hidden[i * SIDE + k])
     part = mm(h[:, :half], own[:, width:], NN) + mm(h[:, half:], other[:, width:], NN)
-    out[...] = part.astype(B)
+    for k in range(SIDE):
+        to = pl.ds(pl.multiple_of(lax.rem(y[0] + k, SIDE) * rows, 16), rows)
+        out[to] = part[k * rows : (k + 1) * rows].astype(B)
 
 
 def spread_over(x, axes):
@@ -134,16 +137,20 @@
         back_kernel, [((ranks, 2, rows, lanes), B), ((rows, lanes), B)], spread_over(parts, ROW)
     )
     grads = spread_over(spread, ROW)
-    hidden = lax.all_gather(hidden, ROW, axis=0, tiled=False)
+    turns = ([(i, (i - k) % SIDE) for i in range(SIDE)] for k in (1, 2, 3))
+    hidden = [hidden] + [lax.ppermute(hidden, "y", t) for t in turns]
+    grads, hidden = lax.optimization_barrier((grads, hidden))
 
     rest, mine = (
         call(functools.partial(input_kernel, h), ((half, width), F), grads, *held[:2]) for h in (1, 0)
     )
     part = (mine + lax.ppermute(rest, "c", SWAP)).astype(B)
-    part = spread_over(part.reshape(depth, half // depth, width), "z")
+    part, hidden = lax.optimization_barrier((part.reshape(depth, half // depth, width), jnp.stack(hidden)))
+    part = spread_over(part, "z")
+    hidden = lax.all_gather(hidden, "x", axis=0, tiled=True)
     grad_input = jnp.sum(part.astype(F), 0).astype(B)
     grad_gate_w, grad_up_w = call(gate_up_kernel, [((hid, width), B)] * 2, grads, own, other)
-    grad_down_w = call(down_kernel, ((hid, width), B), hidden, own, other)
+    grad_down_w = call(down_kernel, ((hid, width), B), hidden, own, other, lax.axis_index("y").reshape(1))
     return (grad_input, grad_gate_w.T, grad_up_w.T, grad_down_w)
 
 

time: 153 us -> 148 us (0.967)
  blocking collectives: 127 us -> 90.2 us
  starting transfers between devices: 12.7 us -> 27 us
  waiting for transfers between devices: 1.15 us -> 15.1 us
    all_to_all x2 -> x1, blocking collectives: 67.6 us -> 40.7 us  [spread_over(): return lax.all_to_all(x, axes, split_axis=0, concat_axis=0, tiled=True)]
    ppermute x0 -> x3, waiting for transfers between devices: none -> 11.6 us  [per_device(): hidden = [hidden] + [lax.ppermute(hidden, 'y', t) for t in turns]]
    ppermute x0 -> x3, starting transfers between devices: none -> 10.5 us  [per_device(): hidden = [hidden] + [lax.ppermute(hidden, 'y', t) for t in turns]]
    all_gather x1, blocking collectives: 23.1 us -> 13.4 us  [per_device(): hidden = lax.all_gather(hidden, 'x', axis=0, tiled=True)]
    all_to_all x1 -> x2, starting transfers between devices: 8.85 us -> 12.6 us  [spread_over(): return lax.all_to_all(x, axes, split_axis=0, concat_axis=0, tiled=True)]
    all_to_all x1 -> x2, waiting for transfers between devices: 0.01 us -> 3.34 us  [spread_over(): return lax.all_to_all(x, axes, split_axis=0, concat_axis=0, tiled=True)]
  transfers between devices with their start and end apart: 3 -> 7, of which waited for: 1 -> 4; matrix products, arithmetic and copies ran while one was open for 0% -> 1% of each run, Pallas kernels for 5% -> 5%
where the time goes in v3:
time: 148 us
  blocking collectives  90.2 us (61%)
  starting transfers between devices  27 us (18%)
  waiting for transfers between devices  15.1 us (10%)
  Pallas kernels  10.2 us (7%)
  other arithmetic  3.08 us (2%)
    all_to_all x1, blocking collectives, spread_over(): return lax.all_to_all(x, axes, split_axis=0, concat_axis=0, tiled=True)  40.7 us
    all_gather x1, blocking collectives, per_device(): lax.all_gather(jnp.concatenate([tokens, out_grad], 1), 'z', axis=0, tiled...  36.1 us
    all_gather x1, blocking collectives, per_device(): hidden = lax.all_gather(hidden, 'x', axis=0, tiled=True)  13.4 us
    all_to_all x2, starting transfers between devices, spread_over(): return lax.all_to_all(x, axes, split_axis=0, concat_axis=0, tiled=True)  12.6 us
    ppermute x3, waiting for transfers between devices, per_device(): hidden = [hidden] + [lax.ppermute(hidden, 'y', t) for t in turns]  11.6 us
    ppermute x3, starting transfers between devices, per_device(): hidden = [hidden] + [lax.ppermute(hidden, 'y', t) for t in turns]  10.5 us
    pallas_call x7, Pallas kernels, call(): pl.pallas_call(body, out_shape=shapes, in_specs=[pl.BlockSpec(memory_spac...  10.2 us
    all_to_all x2, waiting for transfers between devices, spread_over(): return lax.all_to_all(x, axes, split_axis=0, concat_axis=0, tiled=True)  3.34 us
  transfers between devices with their start and end apart: 7, of which 4 were waited for; matrix products, arithmetic and copies ran while one was open for 1% of the time, Pallas kernels for 5%

profile of v3, /device:TPU:32, one launch (start us, length us, event | category | flops | bytes accessed | tf_op | source)
XLA Modules:
  0.0 147.8 jit_solution(11470330377968184454)
XLA Ops:
  0.6 0.7 pad_maximum_fusion.1
  1.4 36.1 %all_gather.6.own = bf16[256,1024]{1,0:T(8,128)(2,1)S(1)} all-gather(bf16[16,1024]{1,0:T(8,128)(2,1)S(1)} %pad_maximum_fusion.1), channel_id=1, replica_groups=mesh['x'=4,'y'=4,'z'=16,'c'=2] {'z'}, dimensions={0}, use_global_device_ids=true | all-gather | bytes 557056 | tf_op jit(solution)/shard_map/all_gather | solution.py:121
  37.4 0.0 copy-start
  37.4 1.9 %collective-permute-start = (bf16[256,1024]{1,0:T(8,128)(2,1)S(1)}, bf16[256,1024]{1,0:T(8,128)(2,1)S(1)}, u32[]{:S(2)}, u32[]{:S(2)}) collective-permute-start(bf16[256,1024]{1,0:T(8,128)(2,1)S(1)} %all_gather.6.own), channel_id=1, source_target_pairs={{0,1},{1,0},{2,3},{3,2},{4,5},{5,4},{6,7},{7,6},{8,9},{9,8},{10,11... | collective-permute-start | bytes 1572872 | tf_op jit(solution)/shard_map/ppermute | solution.py:122
  39.4 2.6 %shard_map.84 = (bf16[8,3,208,128]{3,2,1,0:T(8,128)(2,1)S(1)}, bf16[832,512]{1,0:T(8,128)(2,1)S(1)}, bf16[832,512]{1,0:T(8,128)(2,1)S(1)}, bf16[832,512]{1,0:T(8,128)(2,1)S(1)}) custom-call(bf16[832,512]{1,0:T(8,128)(2,1)} %bitcast.13, bf16[832,512]{1,0:T(8,128)(2,1)} %bitcast.14, bf16[832,512]{1,0:T(8,128)(2,1)} %wd.1, bf16[256,1024]{1,0:T(8,128)(2,1)S(1)} %all_gather.6.own), custom_call_target="tpu_custom_call" | custom-call | flops 1073741824 | bytes 4194304 | tf_op jit(solution)/shard_map/pallas_call | solution.py:21
  41.9 0.0 copy-done
  41.9 0.0 collective-permute-done.other
  41.9 1.0 shard_map.85
  42.9 0.0 copy-start.2
  42.9 0.8 copy-done.2
  43.7 40.7 %all_to_all.15.got = bf16[16,3,208,128]{3,2,1,0:T(8,128)(2,1)S(1)} all-to-all(bf16[16,3,208,128]{3,2,1,0:T(8,128)(2,1)S(1)} %shard_map.85), channel_id=1, replica_groups=mesh['x'=4,'y'=4,'z'=16,'c'=2] {'x','y'}, dimensions={0} | all-to-all | bytes 5111808 | tf_op jit(solution)/shard_map/all_to_all | solution.py:115
  84.4 1.6 %shard_map.86 = (bf16[16,2,208,128]{3,2,1,0:T(8,128)(2,1)}, bf16[208,128]{1,0:T(8,128)(2,1)S(1)}) custom-call(bf16[16,3,208,128]{3,2,1,0:T(8,128)(2,1)S(1)} %all_to_all.15.got), custom_call_target="tpu_custom_call" | custom-call | flops 1073741824 | bytes 4194304 | tf_op jit(solution)/shard_map/pallas_call | solution.py:21
  86.1 3.7 %all-to-all-start.1 = ((bf16[16,2,208,128]{3,2,1,0:T(8,128)(2,1)}), bf16[16,2,208,128]{3,2,1,0:T(8,128)(2,1)S(1)}, u32[]{:S(2)}, u32[]{:S(2)}) async-start(bf16[16,2,208,128]{3,2,1,0:T(8,128)(2,1)} %get-tuple-element.23), calls=%async_computation.1 | async-start | bytes 3407872 | tf_op jit(solution)/shard_map/all_to_all | solution.py:115
  89.8 4.9 %collective-permute-start.1 = (bf16[208,128]{1,0:T(8,128)(2,1)S(1)}, bf16[208,128]{1,0:T(8,128)(2,1)S(1)}, u32[]{:S(2)}, u32[]{:S(2)}) collective-permute-start(bf16[208,128]{1,0:T(8,128)(2,1)S(1)} %get-tuple-element.26), channel_id=1, source_target_pairs={{0,96},{32,0},{64,32},{96,64},{1,97},{33,1},{65,33},{97,65},{2,98}... | collective-permute-start | bytes 159752 | tf_op jit(solution)/shard_map/ppermute | solution.py:141
  94.7 2.8 %collective-permute-start.2 = (bf16[208,128]{1,0:T(8,128)(2,1)S(1)}, bf16[208,128]{1,0:T(8,128)(2,1)S(1)}, u32[]{:S(2)}, u32[]{:S(2)}) collective-permute-start(bf16[208,128]{1,0:T(8,128)(2,1)S(1)} %get-tuple-element.26), channel_id=1, source_target_pairs={{0,64},{32,96},{64,0},{96,32},{1,65},{33,97},{65,1},{97,33},{2,66}... | collective-permute-start | bytes 159752 | tf_op jit(solution)/shard_map/ppermute | solution.py:141
  97.5 2.8 %collective-permute-start.3 = (bf16[208,128]{1,0:T(8,128)(2,1)S(1)}, bf16[208,128]{1,0:T(8,128)(2,1)}, u32[]{:S(2)}, u32[]{:S(2)}) collective-permute-start(bf16[208,128]{1,0:T(8,128)(2,1)S(1)} %get-tuple-element.26), channel_id=1, source_target_pairs={{0,32},{32,64},{64,96},{96,0},{1,33},{33,65},{65,97},{97,1},{2,34}... | collective-permute-start | bytes 159752 | tf_op jit(solution)/shard_map/ppermute | solution.py:141
  100.2 11.6 %collective-permute-done.1 = bf16[208,128]{1,0:T(8,128)(2,1)S(1)} collective-permute-done((bf16[208,128]{1,0:T(8,128)(2,1)S(1)}, bf16[208,128]{1,0:T(8,128)(2,1)S(1)}, u32[]{:S(2)}, u32[]{:S(2)}) %collective-permute-start.1) | collective-permute-done | bytes 53280 | tf_op jit(solution)/shard_map/ppermute | solution.py:141
  111.8 0.0 collective-permute-done.2
  111.9 0.0 copy-start.4
  111.9 0.6 copy-done.4
  112.5 0.0 collective-permute-done.3
  112.5 1.9 %all-to-all-done.1.grads = bf16[16,2,208,128]{3,2,1,0:T(8,128)(2,1)S(1)} async-done(((bf16[16,2,208,128]{3,2,1,0:T(8,128)(2,1)}), bf16[16,2,208,128]{3,2,1,0:T(8,128)(2,1)S(1)}, u32[]{:S(2)}, u32[]{:S(2)}) %all-to-all-start.1) | async-done | bytes 1703968 | tf_op jit(solution)/shard_map/all_to_all | solution.py:115
  114.3 0.7 shard_map.88
  115.1 0.0 copy-start.5
  115.1 2.1 %collective-permute-start.4 = (f32[256,512]{1,0:T(8,128)S(1)}, f32[256,512]{1,0:T(8,128)S(1)}, u32[]{:S(2)}, u32[]{:S(2)}) collective-permute-start(f32[256,512]{1,0:T(8,128)S(1)} %shard_map.88), channel_id=1, source_target_pairs={{0,1},{1,0},{2,3},{3,2},{4,5},{5,4},{6,7},{7,6},{8,9},{9,8},{10,11... | collective-permute-start | bytes 1572872 | tf_op jit(solution)/shard_map/ppermute | solution.py:147
  117.1 0.7 shard_map.87
  117.9 0.0 copy-start.1
  117.9 0.0 copy-start.3
  117.9 0.0 copy-done.5
  117.9 0.9 pad_maximum_fusion
  118.8 0.2 collective-permute-done.4
  119.0 0.8 add_convert_fusion
  119.8 8.9 %all-to-all-start.2 = ((bf16[16,16,512]{2,1,0:T(8,128)(2,1)}), bf16[16,16,512]{2,1,0:T(8,128)(2,1)S(1)}, u32[]{:S(2)}, u32[]{:S(2)}) async-start(bf16[16,16,512]{2,1,0:T(8,128)(2,1)} %bitcast.2), calls=%async_computation.2 | async-start | bytes 524288 | tf_op jit(solution)/shard_map/all_to_all | solution.py:115
  128.6 0.0 copy-done.1
  128.7 0.0 copy-done.3
  128.7 2.1 %shard_map.89 = (bf16[832,512]{1,0:T(8,128)(2,1)}, bf16[832,512]{1,0:T(8,128)(2,1)}) custom-call(bf16[16,2,208,128]{3,2,1,0:T(8,128)(2,1)S(1)} %all-to-all-done.1.grads, bf16[256,1024]{1,0:T(8,128)(2,1)S(1)} %copy-done.1, bf16[256,1024]{1,0:T(8,128)(2,1)S(1)} %copy-done.3), custom_call_target="tpu_custom_call" | custom-call | flops 1073741824 | bytes 4194304 | tf_op jit(solution)/shard_map/pallas_call | solution.py:21
  130.8 13.4 %all_gather.7.hidden = bf16[16,208,128]{2,1,0:T(8,128)(2,1)S(1)} all-gather(bf16[4,208,128]{2,1,0:T(8,128)(2,1)S(1)} %pad_maximum_fusion), channel_id=1, replica_groups=mesh['x'=4,'y'=4,'z'=16,'c'=2] {'x'}, dimensions={0}, use_global_device_ids=true | all-gather | bytes 1064960 | tf_op jit(solution)/shard_map/all_gather | solution.py:150
  144.2 1.5 %shard_map.90 = bf16[832,512]{1,0:T(8,128)(2,1)} custom-call(bf16[16,208,128]{2,1,0:T(8,128)(2,1)S(1)} %all_gather.7.hidden, bf16[256,1024]{1,0:T(8,128)(2,1)S(1)} %copy-done.1, bf16[256,1024]{1,0:T(8,128)(2,1)S(1)} %copy-done.3, s32[1]{0:T(128)} %bitcast.9.y), custom_call_target="tpu_custom_call" | custom-call | flops 1073741824 | bytes 4194304 | tf_op jit(solution)/shard_map/pallas_call | solution.py:21
  145.7 1.5 all-to-all-done.2
  147.2 0.6 reduce_sum.12
Async XLA Ops:
  37.4 4.5 %copy-start = (bf16[256,1024]{1,0:T(8,128)(2,1)}, bf16[256,1024]{1,0:T(8,128)(2,1)S(1)}, u32[]{:S(2)}) copy-start(bf16[256,1024]{1,0:T(8,128)(2,1)S(1)} %all_gather.6.own) | copy-start | bytes 1572868
  37.4 4.5 %collective-permute-start = (bf16[256,1024]{1,0:T(8,128)(2,1)S(1)}, bf16[256,1024]{1,0:T(8,128)(2,1)S(1)}, u32[]{:S(2)}, u32[]{:S(2)}) collective-permute-start(bf16[256,1024]{1,0:T(8,128)(2,1)S(1)} %all_gather.6.own), channel_id=1, source_target_pairs={{0,1},{1,0},{2,3},{3,2},{4,5},{5,4},{6,7},{7,6},{8,9},{9,8},{10,11... | collective-permute-start | bytes 1572872 | tf_op jit(solution)/shard_map/ppermute | solution.py:122
  42.9 0.8 copy-start.2
  86.1 28.3 %all-to-all-start.1 = ((bf16[16,2,208,128]{3,2,1,0:T(8,128)(2,1)}), bf16[16,2,208,128]{3,2,1,0:T(8,128)(2,1)S(1)}, u32[]{:S(2)}, u32[]{:S(2)}) async-start(bf16[16,2,208,128]{3,2,1,0:T(8,128)(2,1)} %get-tuple-element.23), calls=%async_computation.1 | async-start | bytes 3407872 | tf_op jit(solution)/shard_map/all_to_all | solution.py:115
  89.8 22.1 %collective-permute-start.1 = (bf16[208,128]{1,0:T(8,128)(2,1)S(1)}, bf16[208,128]{1,0:T(8,128)(2,1)S(1)}, u32[]{:S(2)}, u32[]{:S(2)}) collective-permute-start(bf16[208,128]{1,0:T(8,128)(2,1)S(1)} %get-tuple-element.26), channel_id=1, source_target_pairs={{0,96},{32,0},{64,32},{96,64},{1,97},{33,1},{65,33},{97,65},{2,98}... | collective-permute-start | bytes 159752 | tf_op jit(solution)/shard_map/ppermute | solution.py:141
  94.7 17.1 %collective-permute-start.2 = (bf16[208,128]{1,0:T(8,128)(2,1)S(1)}, bf16[208,128]{1,0:T(8,128)(2,1)S(1)}, u32[]{:S(2)}, u32[]{:S(2)}) collective-permute-start(bf16[208,128]{1,0:T(8,128)(2,1)S(1)} %get-tuple-element.26), channel_id=1, source_target_pairs={{0,64},{32,96},{64,0},{96,32},{1,65},{33,97},{65,1},{97,33},{2,66}... | collective-permute-start | bytes 159752 | tf_op jit(solution)/shard_map/ppermute | solution.py:141
  97.5 15.0 %collective-permute-start.3 = (bf16[208,128]{1,0:T(8,128)(2,1)S(1)}, bf16[208,128]{1,0:T(8,128)(2,1)}, u32[]{:S(2)}, u32[]{:S(2)}) collective-permute-start(bf16[208,128]{1,0:T(8,128)(2,1)S(1)} %get-tuple-element.26), channel_id=1, source_target_pairs={{0,32},{32,64},{64,96},{96,0},{1,33},{33,65},{65,97},{97,1},{2,34}... | collective-permute-start | bytes 159752 | tf_op jit(solution)/shard_map/ppermute | solution.py:141
  111.9 0.6 copy-start.4
  115.1 2.8 %copy-start.5 = (bf16[208,128]{1,0:T(8,128)(2,1)S(1)}, bf16[208,128]{1,0:T(8,128)(2,1)}, u32[]{:S(2)}) copy-start(bf16[208,128]{1,0:T(8,128)(2,1)} %copy-done.4) | copy-start | bytes 159748
  115.1 3.9 %collective-permute-start.4 = (f32[256,512]{1,0:T(8,128)S(1)}, f32[256,512]{1,0:T(8,128)S(1)}, u32[]{:S(2)}, u32[]{:S(2)}) collective-permute-start(f32[256,512]{1,0:T(8,128)S(1)} %shard_map.88), channel_id=1, source_target_pairs={{0,1},{1,0},{2,3},{3,2},{4,5},{5,4},{6,7},{7,6},{8,9},{9,8},{10,11... | collective-permute-start | bytes 1572872 | tf_op jit(solution)/shard_map/ppermute | solution.py:147
  117.9 10.8 %copy-start.1 = (bf16[256,1024]{1,0:T(8,128)(2,1)S(1)}, bf16[256,1024]{1,0:T(8,128)(2,1)}, u32[]{:S(2)}) copy-start(bf16[256,1024]{1,0:T(8,128)(2,1)} %copy-done) | copy-start | bytes 1572868
  117.9 10.8 %copy-start.3 = (bf16[256,1024]{1,0:T(8,128)(2,1)S(1)}, bf16[256,1024]{1,0:T(8,128)(2,1)}, u32[]{:S(2)}) copy-start(bf16[256,1024]{1,0:T(8,128)(2,1)} %copy-done.2) | copy-start | bytes 1572868
  119.8 27.4 %all-to-all-start.2 = ((bf16[16,16,512]{2,1,0:T(8,128)(2,1)}), bf16[16,16,512]{2,1,0:T(8,128)(2,1)S(1)}, u32[]{:S(2)}, u32[]{:S(2)}) async-start(bf16[16,16,512]{2,1,0:T(8,128)(2,1)} %bitcast.2), calls=%async_computation.2 | async-start | bytes 524288 | tf_op jit(solution)/shard_map/all_to_all | solution.py:115

commit v4 on v2

v4 whole, which is shorter than its diff:
```python
import jax
import jax.numpy as jnp
from jax import lax
from jax.experimental import pallas as pl
from jax.experimental.pallas import tpu as pltpu
from jax.sharding import Mesh, PartitionSpec as P

ROW = ("x", "y")
SWAP = [(0, 1), (1, 0)]
B, F = jnp.bfloat16, jnp.float32
SIDE = 4
NN, NT, TN = ((1,), (0,)), ((1,), (1,)), ((0,), (0,))


def call(body, outs, *args, weights=(), scratch=(), cost=1 << 30):
    many = isinstance(outs, list)
    shapes = [jax.ShapeDtypeStruct(s, d) for s, d in (outs if many else [outs])]
    made = pl.pallas_call(
        body,
        out_shape=shapes,
        in_specs=[pl.BlockSpec(memory_space=pltpu.HBM)] * len(weights)
        + [pl.BlockSpec(memory_space=pltpu.SMEM if a.dtype == jnp.int32 else pltpu.VMEM) for a in args],
        out_specs=[pl.BlockSpec(memory_space=pltpu.VMEM)] * len(shapes),
        scratch_shapes=list(scratch),
        compiler_params=pltpu.CompilerParams(vmem_limit_bytes=24 << 20),
        cost_estimate=pl.CostEstimate(flops=cost, bytes_accessed=cost >> 8, transcendentals=0),
    )(*weights, *args)
    return made if many else made[0]


def mm(a, b, dims):
    return lax.dot_general(a, b, (dims, ((), ())), preferred_element_type=F)


def load_kernel(*refs):
    *weights, held, sems = refs
    copies = [pltpu.make_async_copy(w, held.at[i], sems.at[i]) for i, w in enumerate(weights)]
    for copy in copies:
        copy.start()
    for copy in copies:
        copy.wait()


def parts_kernel(own, held, away, out):
    width, rows, lanes = held.shape[2], out.shape[2], out.shape[3]
    for h, weights in enumerate((held, away)):
        for p in range(3):
            t = own[:, width:] if p == 2 else own[:, :width]
            part = mm(weights[p], t, NT).astype(B)
            for i in range(2):
                for j in range(SIDE):
                    out[(2 * h + i) * SIDE + j, p] = part[j * rows : (j + 1) * rows, i * lanes : (i + 1) * lanes]


def back_kernel(got, spread):
    gate, up, back = (sum(got[r, i].astype(F) for r in range(got.shape[0])) for i in range(3))
    sig = jax.nn.sigmoid(gate)
    active = gate * sig
    hidden = (active * up).astype(B)
    grad_gate = (back * up * sig * (1.0 + gate * (1.0 - sig))).astype(B)
    grad_up = (back * active).astype(B)
    for r in range(spread.shape[0]):
        spread[r, 0] = grad_gate
        spread[r, 1] = grad_up
        spread[r, 2] = hidden


def all_of(blocks):
    return jnp.concatenate([jnp.concatenate([blocks(i, j) for j in range(SIDE)], 0) for i in range(2)], 1)


def input_kernel(grads, held, away, out):
    out[...] = sum(
        mm(all_of(lambda i, j: grads[(2 * h + i) * SIDE + j, p]), weights[p], TN)
        for h, weights in enumerate((held, away))
        for p in range(2)
    ).astype(B)


def send_kernel(grads, out):
    out[...] = grads[out.shape[0] :]


def products_of(grads, tokens):
    width = tokens.shape[1] // 2
    for p in range(3):
        cut = slice(width, None) if p == 2 else slice(None, width)
        yield mm(all_of(lambda i, j: grads[i * SIDE + j, p]), tokens[:, cut], NN)


def own_weight_kernel(grads, own, out):
    for p, part in enumerate(products_of(grads, own)):
        out[p] = part


def weight_kernel(first, got, other, *outs):
    for p, part in enumerate(products_of(got, other)):
        outs[p][...] = (first[p] + part).astype(B)


def spread_over(x, axes):
    return lax.all_to_all(x, axes, split_axis=0, concat_axis=0, tiled=True)


def swapped(x):
    return lax.ppermute(x, "c", SWAP)


def per_device(tokens, out_grad, w_gate, w_up, w_down):
    hid, width = w_down.shape
    depth = lax.axis_size("z")
    weights = [pltpu.with_memory_space_constraint(w, pltpu.HBM) for w in (w_gate.T, w_up.T, w_down)]
    held = call(load_kernel, ((3, hid, width), B), weights=weights, scratch=[pltpu.SemaphoreType.DMA((3,))])
    away = swapped(held)
    mine, held = lax.optimization_barrier((jnp.concatenate([tokens, out_grad], 1), held))
    own = lax.all_gather(mine, "z", axis=0, tiled=True)
    half = own.shape[0]
    rows, lanes, ranks = hid // SIDE, half // 2, SIDE * SIDE

    sizes = (ranks, 3, rows, lanes)
    parts = call(parts_kernel, (sizes, B), own, held, away)
    spread = call(back_kernel, (sizes, B), spread_over(parts, ROW))
    grads = spread_over(spread, ROW)

    part = call(input_kernel, ((half, width), B), grads, held, away)
    part, grads, own = lax.optimization_barrier((part.reshape(depth, half // depth, width), grads, own))
    part = spread_over(part, "z")
    got = swapped(call(send_kernel, ((ranks // 2,) + sizes[1:], B), grads, cost=256))
    other = swapped(own)
    first = call(own_weight_kernel, ((3, hid, width), F), grads, own, cost=1 << 35)
    grad_gate_w, grad_up_w, grad_down_w = call(
        weight_kernel, [((hid, width), B)] * 3, first, got, other, cost=256
    )
    part, grad_gate_w, grad_up_w, grad_down_w = lax.optimization_barrier(
        (part, grad_gate_w, grad_up_w, grad_down_w)
    )
    grad_input = jnp.sum(part.astype(F), 0).astype(B)
    return (grad_input, grad_gate_w.T, grad_up_w.T, grad_down_w)


def solution(mesh):
    shape = (SIDE, SIDE, mesh.devices.shape[1] // 2, 2)
    mesh = Mesh(mesh.devices.reshape(shape), ("x", "y", "z", "c"))
    col = ("z", "c")
    placed = (P(col, ROW), P(col, ROW), P(ROW, col), P(ROW, col), P(col, ROW))
    return jax.shard_map(
        per_device,
        mesh=mesh,
        in_specs=placed,
        out_specs=(P(col, ROW), P(ROW, col), P(ROW, col), P(col, ROW)),
        check_vma=False,
    )
```

time: 153 us -> 132 us (0.86)
  blocking collectives: 127 us -> 99.4 us
  waiting for transfers between devices: 1.15 us -> 7.51 us
  starting transfers between devices: 12.7 us -> 14.8 us
    all_gather x2 -> x1, blocking collectives: 59.1 us -> 36.3 us  [per_device(): own = lax.all_gather(mine, 'z', axis=0, tiled=True)]
    all_to_all x1, waiting for transfers between devices: 0.01 us -> 5.75 us  [spread_over(): return lax.all_to_all(x, axes, split_axis=0, concat_axis=0, tiled=True)]
    all_to_all x2, blocking collectives: 67.6 us -> 63.2 us  [spread_over(): return lax.all_to_all(x, axes, split_axis=0, concat_axis=0, tiled=True)]
    ppermute x2 -> x3, starting transfers between devices: 3.83 us -> 6.24 us  [swapped(): return lax.ppermute(x, 'c', SWAP)]
  transfers between devices with their start and end apart: 3 -> 4, of which waited for: 1 -> 2; matrix products, arithmetic and copies ran while one was open for 0% -> 0% of each run, Pallas kernels for 5% -> 2%
where the time goes in v4:
time: 132 us
  blocking collectives  99.4 us (75%)
  starting transfers between devices  14.8 us (11%)
  Pallas kernels  8.45 us (6%)
  waiting for transfers between devices  7.51 us (6%)
    all_to_all x2, blocking collectives, spread_over(): return lax.all_to_all(x, axes, split_axis=0, concat_axis=0, tiled=True)  63.2 us
    all_gather x1, blocking collectives, per_device(): own = lax.all_gather(mine, 'z', axis=0, tiled=True)  36.3 us
    all_to_all x1, starting transfers between devices, spread_over(): return lax.all_to_all(x, axes, split_axis=0, concat_axis=0, tiled=True)  8.6 us
    pallas_call x7, Pallas kernels, call(): pl.pallas_call(body, out_shape=shapes, in_specs=[pl.BlockSpec(memory_spac...  8.45 us
    ppermute x3, starting transfers between devices, swapped(): return lax.ppermute(x, 'c', SWAP)  6.24 us
    all_to_all x1, waiting for transfers between devices, spread_over(): return lax.all_to_all(x, axes, split_axis=0, concat_axis=0, tiled=True)  5.75 us
  transfers between devices with their start and end apart: 4, of which 2 were waited for; matrix products, arithmetic and copies ran while one was open for 0% of the time, Pallas kernels for 2%

profile of v4, /device:TPU:32, one launch (start us, length us, event | category | flops | bytes accessed | tf_op | source)
XLA Modules:
  0.0 131.6 jit_solution(6145995004073195266)
XLA Ops:
  0.6 0.0 copy-start
  0.6 0.0 copy-start.1
  0.7 1.7 %shard_map.84.held = bf16[3,832,512]{2,1,0:T(8,128)(2,1)S(1)} custom-call(bf16[832,512]{1,0:T(8,128)(2,1)} %bitcast.5, bf16[832,512]{1,0:T(8,128)(2,1)} %bitcast.6, bf16[832,512]{1,0:T(8,128)(2,1)} %refs_2_.1), custom_call_target="tpu_custom_call" | custom-call | flops 1073741824 | bytes 4194304 | tf_op jit(solution)/shard_map/pallas_call | solution.py:18
  2.4 1.9 %collective-permute-start = (bf16[3,832,512]{2,1,0:T(8,128)(2,1)S(1)}, bf16[3,832,512]{2,1,0:T(8,128)(2,1)S(1)}, u32[]{:S(2)}, u32[]{:S(2)}) collective-permute-start(bf16[3,832,512]{2,1,0:T(8,128)(2,1)S(1)} %shard_map.84.held), channel_id=1, source_target_pairs={{0,1},{1,0},{2,3},{3,2},{4,5},{5,4},{6,7},{7,6},{8,9},{9,8},{10,11... | collective-permute-start | bytes 7667720 | tf_op jit(solution)/shard_map/ppermute | solution.py:106
  4.3 0.0 copy-done
  4.3 0.0 copy-done.1
  4.3 36.3 %all_gather.3.own = bf16[256,1024]{1,0:T(8,128)(2,1)S(1)} all-gather(bf16[16,1024]{1,0:T(8,128)(2,1)S(1)} %pad_maximum_fusion), channel_id=1, replica_groups=mesh['x'=4,'y'=4,'z'=16,'c'=2] {'z'}, dimensions={0}, use_global_device_ids=true | all-gather | bytes 557056 | tf_op jit(solution)/shard_map/all_gather | solution.py:116
  40.6 0.0 collective-permute-done.away
  40.6 1.5 %shard_map.85 = bf16[16,3,208,128]{3,2,1,0:T(8,128)(2,1)S(1)} custom-call(bf16[256,1024]{1,0:T(8,128)(2,1)S(1)} %all_gather.3.own, bf16[3,832,512]{2,1,0:T(8,128)(2,1)S(1)} %shard_map.84.held, bf16[3,832,512]{2,1,0:T(8,128)(2,1)S(1)} %collective-permute-done.away), custom_call_target="tpu_custom_call" | custom-call | flops 1073741824 | bytes 4194304 | tf_op jit(solution)/shard_map/pallas_call | solution.py:18
  42.1 33.8 %all_to_all.15.got = bf16[16,3,208,128]{3,2,1,0:T(8,128)(2,1)S(1)} all-to-all(bf16[16,3,208,128]{3,2,1,0:T(8,128)(2,1)S(1)} %shard_map.85), channel_id=1, replica_groups=mesh['x'=4,'y'=4,'z'=16,'c'=2] {'x','y'}, dimensions={0} | all-to-all | bytes 5111808 | tf_op jit(solution)/shard_map/all_to_all | solution.py:102
  75.9 0.5 shard_map.86
  76.4 29.4 %all_to_all.16.grads = bf16[16,3,208,128]{3,2,1,0:T(8,128)(2,1)S(1)} all-to-all(bf16[16,3,208,128]{3,2,1,0:T(8,128)(2,1)S(1)} %shard_map.86), channel_id=1, replica_groups=mesh['x'=4,'y'=4,'z'=16,'c'=2] {'x','y'}, dimensions={0} | all-to-all | bytes 5111808 | tf_op jit(solution)/shard_map/all_to_all | solution.py:102
  105.8 2.0 %shard_map.87 = bf16[256,512]{1,0:T(8,128)(2,1)} custom-call(bf16[16,3,208,128]{3,2,1,0:T(8,128)(2,1)S(1)} %all_to_all.16.grads, bf16[3,832,512]{2,1,0:T(8,128)(2,1)S(1)} %shard_map.84.held, bf16[3,832,512]{2,1,0:T(8,128)(2,1)S(1)} %collective-permute-done.away), custom_call_target="tpu_custom_call" | custom-call | flops 1073741824 | bytes 4194304 | tf_op jit(solution)/shard_map/pallas_call | solution.py:18
  107.7 8.6 %all-to-all-start.2 = ((bf16[16,16,512]{2,1,0:T(8,128)(2,1)}), bf16[16,16,512]{2,1,0:T(8,128)(2,1)S(1)}, u32[]{:S(2)}, u32[]{:S(2)}) async-start(bf16[16,16,512]{2,1,0:T(8,128)(2,1)} %bitcast.2), calls=%async_computation.2 | async-start | bytes 524288 | tf_op jit(solution)/shard_map/all_to_all | solution.py:102
  116.3 1.9 %collective-permute-start.2 = (bf16[256,1024]{1,0:T(8,128)(2,1)S(1)}, bf16[256,1024]{1,0:T(8,128)(2,1)S(1)}, u32[]{:S(2)}, u32[]{:S(2)}) collective-permute-start(bf16[256,1024]{1,0:T(8,128)(2,1)S(1)} %all_gather.3.own), channel_id=1, source_target_pairs={{0,1},{1,0},{2,3},{3,2},{4,5},{5,4},{6,7},{7,6},{8,9},{9,8},{10,11... | collective-permute-start | bytes 1572872 | tf_op jit(solution)/shard_map/ppermute | solution.py:106
  118.3 0.1 shard_map.89
  118.4 2.4 %collective-permute-start.1 = (bf16[8,3,208,128]{3,2,1,0:T(8,128)(2,1)S(1)}, bf16[8,3,208,128]{3,2,1,0:T(8,128)(2,1)S(1)}, u32[]{:S(2)}, u32[]{:S(2)}) collective-permute-start(bf16[8,3,208,128]{3,2,1,0:T(8,128)(2,1)S(1)} %shard_map.89), channel_id=1, source_target_pairs={{0,1},{1,0},{2,3},{3,2},{4,5},{5,4},{6,7},{7,6},{8,9},{9,8},{10,11... | collective-permute-start | bytes 3833864 | tf_op jit(solution)/shard_map/ppermute | solution.py:106
  120.8 0.8 shard_map.88.first
  121.6 0.0 collective-permute-done.2.other
  121.6 1.8 %collective-permute-done.1.got = bf16[8,3,208,128]{3,2,1,0:T(8,128)(2,1)S(1)} collective-permute-done((bf16[8,3,208,128]{3,2,1,0:T(8,128)(2,1)S(1)}, bf16[8,3,208,128]{3,2,1,0:T(8,128)(2,1)S(1)}, u32[]{:S(2)}, u32[]{:S(2)}) %collective-permute-start.1) | collective-permute-done | bytes 1277984 | tf_op jit(solution)/shard_map/ppermute | solution.py:106
  123.4 1.9 %shard_map.90 = (bf16[832,512]{1,0:T(8,128)(2,1)}, bf16[832,512]{1,0:T(8,128)(2,1)}, bf16[832,512]{1,0:T(8,128)(2,1)}) custom-call(f32[3,832,512]{2,1,0:T(8,128)S(1)} %shard_map.88.first, bf16[8,3,208,128]{3,2,1,0:T(8,128)(2,1)S(1)} %collective-permute-done.1.got, bf16[256,1024]{1,0:T(8,128)(2,1)S(1)} %collective-permute-done.2.other), custom_call_target="tpu_custom_call" | custom-call | flops 256 | bytes 1 | tf_op jit(solution)/shard_map/pallas_call | solution.py:18
  125.2 5.8 %all-to-all-done.2 = bf16[16,16,512]{2,1,0:T(8,128)(2,1)S(1)} async-done(((bf16[16,16,512]{2,1,0:T(8,128)(2,1)}), bf16[16,16,512]{2,1,0:T(8,128)(2,1)S(1)}, u32[]{:S(2)}, u32[]{:S(2)}) %all-to-all-start.2) | async-done | bytes 262176 | tf_op jit(solution)/shard_map/all_to_all | solution.py:102
  131.0 0.6 reduce_sum.12
  (1 shorter events, 0.0 us)
Async XLA Ops:
  0.6 3.7 %copy-start = (bf16[16,512]{1,0:T(8,128)(2,1)S(1)}, bf16[16,512]{1,0:T(8,128)(2,1)}, u32[]{:S(2)}) copy-start(bf16[16,512]{1,0:T(8,128)(2,1)} %param.6) | copy-start | bytes 49156
  0.6 3.7 %copy-start.1 = (bf16[16,512]{1,0:T(8,128)(2,1)S(1)}, bf16[16,512]{1,0:T(8,128)(2,1)}, u32[]{:S(2)}) copy-start(bf16[16,512]{1,0:T(8,128)(2,1)} %param.5) | copy-start | bytes 49156
  2.4 38.2 %collective-permute-start = (bf16[3,832,512]{2,1,0:T(8,128)(2,1)S(1)}, bf16[3,832,512]{2,1,0:T(8,128)(2,1)S(1)}, u32[]{:S(2)}, u32[]{:S(2)}) collective-permute-start(bf16[3,832,512]{2,1,0:T(8,128)(2,1)S(1)} %shard_map.84.held), channel_id=1, source_target_pairs={{0,1},{1,0},{2,3},{3,2},{4,5},{5,4},{6,7},{7,6},{8,9},{9,8},{10,11... | collective-permute-start | bytes 7667720 | tf_op jit(solution)/shard_map/ppermute | solution.py:106
  107.7 23.2 %all-to-all-start.2 = ((bf16[16,16,512]{2,1,0:T(8,128)(2,1)}), bf16[16,16,512]{2,1,0:T(8,128)(2,1)S(1)}, u32[]{:S(2)}, u32[]{:S(2)}) async-start(bf16[16,16,512]{2,1,0:T(8,128)(2,1)} %bitcast.2), calls=%async_computation.2 | async-start | bytes 524288 | tf_op jit(solution)/shard_map/all_to_all | solution.py:102
  116.3 5.3 %collective-permute-start.2 = (bf16[256,1024]{1,0:T(8,128)(2,1)S(1)}, bf16[256,1024]{1,0:T(8,128)(2,1)S(1)}, u32[]{:S(2)}, u32[]{:S(2)}) collective-permute-start(bf16[256,1024]{1,0:T(8,128)(2,1)S(1)} %all_gather.3.own), channel_id=1, source_target_pairs={{0,1},{1,0},{2,3},{3,2},{4,5},{5,4},{6,7},{7,6},{8,9},{9,8},{10,11... | collective-permute-start | bytes 1572872 | tf_op jit(solution)/shard_map/ppermute | solution.py:106
  118.4 5.0 %collective-permute-start.1 = (bf16[8,3,208,128]{3,2,1,0:T(8,128)(2,1)S(1)}, bf16[8,3,208,128]{3,2,1,0:T(8,128)(2,1)S(1)}, u32[]{:S(2)}, u32[]{:S(2)}) collective-permute-start(bf16[8,3,208,128]{3,2,1,0:T(8,128)(2,1)S(1)} %shard_map.89), channel_id=1, source_target_pairs={{0,1},{1,0},{2,3},{3,2},{4,5},{5,4},{6,7},{7,6},{8,9},{9,8},{10,11... | collective-permute-start | bytes 3833864 | tf_op jit(solution)/shard_map/ppermute | solution.py:106

commit v5 on v4

--- a/solution.py
+++ b/solution.py
@@ -1,11 +1,16 @@
+import functools
+
+
 import jax
 import jax.numpy as jnp
+import numpy as np
 from jax import lax
 from jax.experimental import pallas as pl
 from jax.experimental.pallas import tpu as pltpu
 from jax.sharding import Mesh, PartitionSpec as P
 
 ROW = ("x", "y")
+ALL = ("x", "y", "z", "c")
 SWAP = [(0, 1), (1, 0)]
 B, F = jnp.bfloat16, jnp.float32
 SIDE = 4
@@ -102,11 +107,24 @@
     return lax.all_to_all(x, axes, split_axis=0, concat_axis=0, tiled=True)
 
 
+PATH = [(0, 0), (0, 1), (0, 2), (0, 3), (1, 3), (1, 2), (1, 1), (2, 1)]
+PATH += [(2, 2), (2, 3), (3, 3), (3, 2), (3, 1), (3, 0), (2, 0), (1, 0)]
+
+
+def rows_of(shape):
+    ids = np.arange(int(np.prod(shape))).reshape(shape)
+    return [[int(ids[x, y, z, c]) for x, y in PATH] for z in range(shape[2]) for c in range(2)]
+
+
+def over_rows(v, shape):
+    return lax.all_to_all(v, ALL, split_axis=0, concat_axis=0, tiled=True, axis_index_groups=rows_of(shape))
+
+
 def swapped(x):
     return lax.ppermute(x, "c", SWAP)
 
 
-def per_device(tokens, out_grad, w_gate, w_up, w_down):
+def per_device(shape, tokens, out_grad, w_gate, w_up, w_down):
     hid, width = w_down.shape
     depth = lax.axis_size("z")
     weights = [pltpu.with_memory_space_constraint(w, pltpu.HBM) for w in (w_gate.T, w_up.T, w_down)]
@@ -119,8 +137,8 @@
 
     sizes = (ranks, 3, rows, lanes)
     parts = call(parts_kernel, (sizes, B), own, held, away)
-    spread = call(back_kernel, (sizes, B), spread_over(parts, ROW))
-    grads = spread_over(spread, ROW)
+    spread = call(back_kernel, (sizes, B), over_rows(parts, shape))
+    grads = over_rows(spread, shape)
 
     part = call(input_kernel, ((half, width), B), grads, held, away)
     part, grads, own = lax.optimization_barrier((part.reshape(depth, half // depth, width), grads, own))
@@ -140,11 +158,11 @@
 
 def solution(mesh):
     shape = (SIDE, SIDE, mesh.devices.shape[1] // 2, 2)
-    mesh = Mesh(mesh.devices.reshape(shape), ("x", "y", "z", "c"))
+    mesh = Mesh(mesh.devices.reshape(shape), ALL)
     col = ("z", "c")
     placed = (P(col, ROW), P(col, ROW), P(ROW, col), P(ROW, col), P(col, ROW))
     return jax.shard_map(
-        per_device,
+        functools.partial(per_device, shape),
         mesh=mesh,
         in_specs=placed,
         out_specs=(P(col, ROW), P(ROW, col), P(ROW, col), P(col, ROW)),

time: 132 us -> 131 us (level)
  no operation moved by 1% of the time
where the time goes in v5:
time: 131 us
  blocking collectives  98.2 us (75%)
  starting transfers between devices  15.1 us (12%)
  Pallas kernels  8.45 us (6%)
  waiting for transfers between devices  7.38 us (6%)
    all_to_all x2, blocking collectives, over_rows(): lax.all_to_all(v, ALL, split_axis=0, concat_axis=0, tiled=True, axis_inde...  62 us
    all_gather x1, blocking collectives, per_device(): own = lax.all_gather(mine, 'z', axis=0, tiled=True)  36.3 us
    all_to_all x1, starting transfers between devices, spread_over(): return lax.all_to_all(x, axes, split_axis=0, concat_axis=0, tiled=True)  8.89 us
    pallas_call x7, Pallas kernels, call(): pl.pallas_call(body, out_shape=shapes, in_specs=[pl.BlockSpec(memory_spac...  8.45 us
    ppermute x3, starting transfers between devices, swapped(): return lax.ppermute(x, 'c', SWAP)  6.24 us
    all_to_all x1, waiting for transfers between devices, spread_over(): return lax.all_to_all(x, axes, split_axis=0, concat_axis=0, tiled=True)  5.62 us
  transfers between devices with their start and end apart: 4, of which 2 were waited for; matrix products, arithmetic and copies ran while one was open for 0% of the time, Pallas kernels for 2%

profile of v5, /device:TPU:32, one launch (start us, length us, event | category | flops | bytes accessed | tf_op | source)
XLA Modules:
  0.0 130.6 jit_solution(6849887964765354839)
XLA Ops:
  0.6 0.0 copy-start
  0.6 0.0 copy-start.1
  0.7 1.7 %shard_map.84.held = bf16[3,832,512]{2,1,0:T(8,128)(2,1)S(1)} custom-call(bf16[832,512]{1,0:T(8,128)(2,1)} %bitcast.5, bf16[832,512]{1,0:T(8,128)(2,1)} %bitcast.6, bf16[832,512]{1,0:T(8,128)(2,1)} %refs_2_.1), custom_call_target="tpu_custom_call" | custom-call | flops 1073741824 | bytes 4194304 | tf_op jit(solution)/shard_map/pallas_call | solution.py:23
  2.4 1.9 %collective-permute-start = (bf16[3,832,512]{2,1,0:T(8,128)(2,1)S(1)}, bf16[3,832,512]{2,1,0:T(8,128)(2,1)S(1)}, u32[]{:S(2)}, u32[]{:S(2)}) collective-permute-start(bf16[3,832,512]{2,1,0:T(8,128)(2,1)S(1)} %shard_map.84.held), channel_id=1, source_target_pairs={{0,1},{1,0},{2,3},{3,2},{4,5},{5,4},{6,7},{7,6},{8,9},{9,8},{10,11... | collective-permute-start | bytes 7667720 | tf_op jit(solution)/shard_map/ppermute | solution.py:124
  4.3 0.0 copy-done
  4.3 0.0 copy-done.1
  4.3 36.3 %all_gather.3.own = bf16[256,1024]{1,0:T(8,128)(2,1)S(1)} all-gather(bf16[16,1024]{1,0:T(8,128)(2,1)S(1)} %pad_maximum_fusion), channel_id=1, replica_groups=mesh['x'=4,'y'=4,'z'=16,'c'=2] {'z'}, dimensions={0}, use_global_device_ids=true | all-gather | bytes 557056 | tf_op jit(solution)/shard_map/all_gather | solution.py:134
  40.6 0.0 collective-permute-done.away
  40.6 1.5 %shard_map.85 = bf16[16,3,208,128]{3,2,1,0:T(8,128)(2,1)S(1)} custom-call(bf16[256,1024]{1,0:T(8,128)(2,1)S(1)} %all_gather.3.own, bf16[3,832,512]{2,1,0:T(8,128)(2,1)S(1)} %shard_map.84.held, bf16[3,832,512]{2,1,0:T(8,128)(2,1)S(1)} %collective-permute-done.away), custom_call_target="tpu_custom_call" | custom-call | flops 1073741824 | bytes 4194304 | tf_op jit(solution)/shard_map/pallas_call | solution.py:23
  42.1 33.2 %all_to_all.15.got = bf16[16,3,208,128]{3,2,1,0:T(8,128)(2,1)S(1)} all-to-all(bf16[16,3,208,128]{3,2,1,0:T(8,128)(2,1)S(1)} %shard_map.85), channel_id=1, replica_groups={{0,32,64,96,224,192,160,288,320,352,480,448,416,384,256,128},{1,33,65,9..., dimensions={0} | all-to-all | bytes 5111808 | tf_op jit(solution)/shard_map/all_to_all | solution.py:120
  75.3 0.5 shard_map.86
  75.8 28.8 %all_to_all.16.grads = bf16[16,3,208,128]{3,2,1,0:T(8,128)(2,1)S(1)} all-to-all(bf16[16,3,208,128]{3,2,1,0:T(8,128)(2,1)S(1)} %shard_map.86), channel_id=1, replica_groups={{0,32,64,96,224,192,160,288,320,352,480,448,416,384,256,128},{1,33,65,9..., dimensions={0} | all-to-all | bytes 5111808 | tf_op jit(solution)/shard_map/all_to_all | solution.py:120
  104.6 2.0 %shard_map.87 = bf16[256,512]{1,0:T(8,128)(2,1)} custom-call(bf16[16,3,208,128]{3,2,1,0:T(8,128)(2,1)S(1)} %all_to_all.16.grads, bf16[3,832,512]{2,1,0:T(8,128)(2,1)S(1)} %shard_map.84.held, bf16[3,832,512]{2,1,0:T(8,128)(2,1)S(1)} %collective-permute-done.away), custom_call_target="tpu_custom_call" | custom-call | flops 1073741824 | bytes 4194304 | tf_op jit(solution)/shard_map/pallas_call | solution.py:23
  106.6 8.9 %all-to-all-start.2 = ((bf16[16,16,512]{2,1,0:T(8,128)(2,1)}), bf16[16,16,512]{2,1,0:T(8,128)(2,1)S(1)}, u32[]{:S(2)}, u32[]{:S(2)}) async-start(bf16[16,16,512]{2,1,0:T(8,128)(2,1)} %bitcast.2), calls=%async_computation.2 | async-start | bytes 524288 | tf_op jit(solution)/shard_map/all_to_all | solution.py:107
  115.4 1.9 %collective-permute-start.2 = (bf16[256,1024]{1,0:T(8,128)(2,1)S(1)}, bf16[256,1024]{1,0:T(8,128)(2,1)S(1)}, u32[]{:S(2)}, u32[]{:S(2)}) collective-permute-start(bf16[256,1024]{1,0:T(8,128)(2,1)S(1)} %all_gather.3.own), channel_id=1, source_target_pairs={{0,1},{1,0},{2,3},{3,2},{4,5},{5,4},{6,7},{7,6},{8,9},{9,8},{10,11... | collective-permute-start | bytes 1572872 | tf_op jit(solution)/shard_map/ppermute | solution.py:124
  117.4 0.1 shard_map.89
  117.5 2.4 %collective-permute-start.1 = (bf16[8,3,208,128]{3,2,1,0:T(8,128)(2,1)S(1)}, bf16[8,3,208,128]{3,2,1,0:T(8,128)(2,1)S(1)}, u32[]{:S(2)}, u32[]{:S(2)}) collective-permute-start(bf16[8,3,208,128]{3,2,1,0:T(8,128)(2,1)S(1)} %shard_map.89), channel_id=1, source_target_pairs={{0,1},{1,0},{2,3},{3,2},{4,5},{5,4},{6,7},{7,6},{8,9},{9,8},{10,11... | collective-permute-start | bytes 3833864 | tf_op jit(solution)/shard_map/ppermute | solution.py:124
  119.9 0.8 shard_map.88.first
  120.7 0.0 collective-permute-done.2.other
  120.7 1.8 %collective-permute-done.1.got = bf16[8,3,208,128]{3,2,1,0:T(8,128)(2,1)S(1)} collective-permute-done((bf16[8,3,208,128]{3,2,1,0:T(8,128)(2,1)S(1)}, bf16[8,3,208,128]{3,2,1,0:T(8,128)(2,1)S(1)}, u32[]{:S(2)}, u32[]{:S(2)}) %collective-permute-start.1) | collective-permute-done | bytes 1277984 | tf_op jit(solution)/shard_map/ppermute | solution.py:124
  122.5 1.9 %shard_map.90 = (bf16[832,512]{1,0:T(8,128)(2,1)}, bf16[832,512]{1,0:T(8,128)(2,1)}, bf16[832,512]{1,0:T(8,128)(2,1)}) custom-call(f32[3,832,512]{2,1,0:T(8,128)S(1)} %shard_map.88.first, bf16[8,3,208,128]{3,2,1,0:T(8,128)(2,1)S(1)} %collective-permute-done.1.got, bf16[256,1024]{1,0:T(8,128)(2,1)S(1)} %collective-permute-done.2.other), custom_call_target="tpu_custom_call" | custom-call | flops 256 | bytes 1 | tf_op jit(solution)/shard_map/pallas_call | solution.py:23
  124.3 5.6 %all-to-all-done.2 = bf16[16,16,512]{2,1,0:T(8,128)(2,1)S(1)} async-done(((bf16[16,16,512]{2,1,0:T(8,128)(2,1)}), bf16[16,16,512]{2,1,0:T(8,128)(2,1)S(1)}, u32[]{:S(2)}, u32[]{:S(2)}) %all-to-all-start.2) | async-done | bytes 262176 | tf_op jit(solution)/shard_map/all_to_all | solution.py:107
  129.9 0.6 reduce_sum.12
  (1 shorter events, 0.0 us)
Async XLA Ops:
  0.6 3.7 %copy-start = (bf16[16,512]{1,0:T(8,128)(2,1)S(1)}, bf16[16,512]{1,0:T(8,128)(2,1)}, u32[]{:S(2)}) copy-start(bf16[16,512]{1,0:T(8,128)(2,1)} %param.6) | copy-start | bytes 49156
  0.6 3.7 %copy-start.1 = (bf16[16,512]{1,0:T(8,128)(2,1)S(1)}, bf16[16,512]{1,0:T(8,128)(2,1)}, u32[]{:S(2)}) copy-start(bf16[16,512]{1,0:T(8,128)(2,1)} %param.5) | copy-start | bytes 49156
  2.4 38.2 %collective-permute-start = (bf16[3,832,512]{2,1,0:T(8,128)(2,1)S(1)}, bf16[3,832,512]{2,1,0:T(8,128)(2,1)S(1)}, u32[]{:S(2)}, u32[]{:S(2)}) collective-permute-start(bf16[3,832,512]{2,1,0:T(8,128)(2,1)S(1)} %shard_map.84.held), channel_id=1, source_target_pairs={{0,1},{1,0},{2,3},{3,2},{4,5},{5,4},{6,7},{7,6},{8,9},{9,8},{10,11... | collective-permute-start | bytes 7667720 | tf_op jit(solution)/shard_map/ppermute | solution.py:124
  106.6 23.4 %all-to-all-start.2 = ((bf16[16,16,512]{2,1,0:T(8,128)(2,1)}), bf16[16,16,512]{2,1,0:T(8,128)(2,1)S(1)}, u32[]{:S(2)}, u32[]{:S(2)}) async-start(bf16[16,16,512]{2,1,0:T(8,128)(2,1)} %bitcast.2), calls=%async_computation.2 | async-start | bytes 524288 | tf_op jit(solution)/shard_map/all_to_all | solution.py:107
  115.4 5.3 %collective-permute-start.2 = (bf16[256,1024]{1,0:T(8,128)(2,1)S(1)}, bf16[256,1024]{1,0:T(8,128)(2,1)S(1)}, u32[]{:S(2)}, u32[]{:S(2)}) collective-permute-start(bf16[256,1024]{1,0:T(8,128)(2,1)S(1)} %all_gather.3.own), channel_id=1, source_target_pairs={{0,1},{1,0},{2,3},{3,2},{4,5},{5,4},{6,7},{7,6},{8,9},{9,8},{10,11... | collective-permute-start | bytes 1572872 | tf_op jit(solution)/shard_map/ppermute | solution.py:124
  117.5 5.0 %collective-permute-start.1 = (bf16[8,3,208,128]{3,2,1,0:T(8,128)(2,1)S(1)}, bf16[8,3,208,128]{3,2,1,0:T(8,128)(2,1)S(1)}, u32[]{:S(2)}, u32[]{:S(2)}) collective-permute-start(bf16[8,3,208,128]{3,2,1,0:T(8,128)(2,1)S(1)} %shard_map.89), channel_id=1, source_target_pairs={{0,1},{1,0},{2,3},{3,2},{4,5},{5,4},{6,7},{7,6},{8,9},{9,8},{10,11... | collective-permute-start | bytes 3833864 | tf_op jit(solution)/shard_map/ppermute | solution.py:124

commit v6 on v5

--- a/solution.py
+++ b/solution.py
@@ -46,15 +46,25 @@
         copy.wait()
 
 
+def main_of(hid):
+    return hid // 128 * 128
+
+
+def pieces(held, away, p):
+    main = main_of(held.shape[1])
+    return held[p, :main], away[p, :main], jnp.concatenate([held[p, main:], away[p, main:]], 0)
+
+
 def parts_kernel(own, held, away, out):
-    width, rows, lanes = held.shape[2], out.shape[2], out.shape[3]
-    for h, weights in enumerate((held, away)):
-        for p in range(3):
-            t = own[:, width:] if p == 2 else own[:, :width]
-            part = mm(weights[p], t, NT).astype(B)
-            for i in range(2):
-                for j in range(SIDE):
-                    out[(2 * h + i) * SIDE + j, p] = part[j * rows : (j + 1) * rows, i * lanes : (i + 1) * lanes]
+    width, rows = held.shape[2], out.shape[2]
+    for p in range(3):
+        t = own[:, width:] if p == 2 else own[:, :width]
+        start = 0
+        for w in pieces(held, away, p):
+            part = mm(t, w, NT).astype(B)
+            for r in range(out.shape[0]):
+                out[r, p, :, start : start + w.shape[0]] = part[r * rows : (r + 1) * rows]
+            start += w.shape[0]
 
 
 def back_kernel(got, spread):
@@ -70,37 +80,44 @@
         spread[r, 2] = hidden
 
 
-def all_of(blocks):
-    return jnp.concatenate([jnp.concatenate([blocks(i, j) for j in range(SIDE)], 0) for i in range(2)], 1)
+def plane(grads, p):
+    ranks, _, rows, hid = grads.shape
+    return grads[:, p].reshape(ranks * rows, hid)
 
 
 def input_kernel(grads, held, away, out):
-    out[...] = sum(
-        mm(all_of(lambda i, j: grads[(2 * h + i) * SIDE + j, p]), weights[p], TN)
-        for h, weights in enumerate((held, away))
-        for p in range(2)
-    ).astype(B)
+    g = jnp.concatenate([plane(grads, 0), plane(grads, 1)], 1)
+    w = jnp.concatenate([piece for p in range(2) for piece in pieces(held, away, p)], 0)
+    out[...] = mm(g, w, NN).astype(B)
 
 
-def send_kernel(grads, out):
-    out[...] = grads[out.shape[0] :]
-
-
-def products_of(grads, tokens):
-    width = tokens.shape[1] // 2
+def send_kernel(grads, own, out):
+    cut = (out.shape[1] - own.shape[1]) // 3
     for p in range(3):
-        cut = slice(width, None) if p == 2 else slice(None, width)
-        yield mm(all_of(lambda i, j: grads[i * SIDE + j, p]), tokens[:, cut], NN)
+        out[:, p * cut : (p + 1) * cut] = plane(grads, p)[:, cut - 128 :]
+    out[:, 3 * cut :] = own[...]
 
 
 def own_weight_kernel(grads, own, out):
-    for p, part in enumerate(products_of(grads, own)):
-        out[p] = part
+    hid, width = out.shape[1:]
+    main = main_of(hid)
+    for p in range(3):
+        t = own[:, width:] if p == 2 else own[:, :width]
+        g = plane(grads, p)
+        out[p, :main] = mm(g[:, :main], t, TN)
+        out[p, main:] = mm(g[:, 2 * main :], t, TN)[: hid - main]
 
 
-def weight_kernel(first, got, other, *outs):
-    for p, part in enumerate(products_of(got, other)):
-        outs[p][...] = (first[p] + part).astype(B)
+def weight_kernel(first, got, *outs):
+    hid, width = first.shape[1:]
+    main = main_of(hid)
+    cut = main + 128
+    other = 3 * cut
+    for p, out in enumerate(outs):
+        t = got[:, other + width :] if p == 2 else got[:, other : other + width]
+        g = got[:, p * cut : (p + 1) * cut]
+        out[:main] = (first[p, :main] + mm(g[:, :main], t, TN)).astype(B)
+        out[main:] = (first[p, main:] + mm(g[:, main:], t, TN)[hid - main :]).astype(B)
 
 
 def spread_over(x, axes):
@@ -133,9 +150,9 @@
     mine, held = lax.optimization_barrier((jnp.concatenate([tokens, out_grad], 1), held))
     own = lax.all_gather(mine, "z", axis=0, tiled=True)
     half = own.shape[0]
-    rows, lanes, ranks = hid // SIDE, half // 2, SIDE * SIDE
+    ranks = SIDE * SIDE
 
-    sizes = (ranks, 3, rows, lanes)
+    sizes = (ranks, 3, half // ranks, 2 * hid)
     parts = call(parts_kernel, (sizes, B), own, held, away)
     spread = call(back_kernel, (sizes, B), over_rows(parts, shape))
     grads = over_rows(spread, shape)
@@ -143,11 +160,10 @@
     part = call(input_kernel, ((half, width), B), grads, held, away)
     part, grads, own = lax.optimization_barrier((part.reshape(depth, half // depth, width), grads, own))
     part = spread_over(part, "z")
-    got = swapped(call(send_kernel, ((ranks // 2,) + sizes[1:], B), grads, cost=256))
-    other = swapped(own)
+    got = swapped(call(send_kernel, ((half, 3 * (main_of(hid) + 128) + 2 * width), B), grads, own, cost=256))
     first = call(own_weight_kernel, ((3, hid, width), F), grads, own, cost=1 << 35)
     grad_gate_w, grad_up_w, grad_down_w = call(
-        weight_kernel, [((hid, width), B)] * 3, first, got, other, cost=256
+        weight_kernel, [((hid, width), B)] * 3, first, got, cost=256
     )
     part, grad_gate_w, grad_up_w, grad_down_w = lax.optimization_barrier(
         (part, grad_gate_w, grad_up_w, grad_down_w)

time: 131 us -> 131 us (level)
  starting transfers between devices: 15.1 us -> 12.7 us
  waiting for transfers between devices: 7.38 us -> 9.6 us
    ppermute x3 -> x2, starting transfers between devices: 6.24 us -> 3.84 us  [swapped(): return lax.ppermute(x, 'c', SWAP)]
    ppermute x3 -> x2, waiting for transfers between devices: 1.76 us -> 2.94 us  [swapped(): return lax.ppermute(x, 'c', SWAP)]
  transfers between devices with their start and end apart: 4 -> 3, of which waited for: 2 -> 2; matrix products, arithmetic and copies ran while one was open for 0% -> 0% of each run, Pallas kernels for 2% -> 2%
where the time goes in v6:
time: 131 us; the launch traced here: 130 us
  blocking collectives  98.2 us (75%)
  starting transfers between devices  12.7 us (10%)
  waiting for transfers between devices  9.6 us (7%)
  Pallas kernels  8.51 us (6%)
    all_to_all x2, blocking collectives, over_rows(): lax.all_to_all(v, ALL, split_axis=0, concat_axis=0, tiled=True, axis_inde...  62 us
    all_gather x1, blocking collectives, per_device(): own = lax.all_gather(mine, 'z', axis=0, tiled=True)  36.3 us
    all_to_all x1, starting transfers between devices, spread_over(): return lax.all_to_all(x, axes, split_axis=0, concat_axis=0, tiled=True)  8.86 us
    pallas_call x7, Pallas kernels, call(): pl.pallas_call(body, out_shape=shapes, in_specs=[pl.BlockSpec(memory_spac...  8.51 us
    all_to_all x1, waiting for transfers between devices, spread_over(): return lax.all_to_all(x, axes, split_axis=0, concat_axis=0, tiled=True)  6.66 us
    ppermute x2, starting transfers between devices, swapped(): return lax.ppermute(x, 'c', SWAP)  3.84 us
    ppermute x2, waiting for transfers between devices, swapped(): return lax.ppermute(x, 'c', SWAP)  2.94 us
  transfers between devices with their start and end apart: 3, of which 2 were waited for; matrix products, arithmetic and copies ran while one was open for 0% of the time, Pallas kernels for 2%

profile of v6, /device:TPU:32, one launch (start us, length us, event | category | flops | bytes accessed | tf_op | source)
XLA Modules:
  0.0 130.4 jit_solution(7501922101711772716)
XLA Ops:
  0.6 0.0 copy-start
  0.6 0.0 copy-start.1
  0.7 1.7 %shard_map.84.held = bf16[3,832,512]{2,1,0:T(8,128)(2,1)S(1)} custom-call(bf16[832,512]{1,0:T(8,128)(2,1)} %bitcast.5, bf16[832,512]{1,0:T(8,128)(2,1)} %bitcast.6, bf16[832,512]{1,0:T(8,128)(2,1)} %refs_2_.1), custom_call_target="tpu_custom_call" | custom-call | flops 1073741824 | bytes 4194304 | tf_op jit(solution)/shard_map/pallas_call | solution.py:23
  2.4 1.9 %collective-permute-start = (bf16[3,832,512]{2,1,0:T(8,128)(2,1)S(1)}, bf16[3,832,512]{2,1,0:T(8,128)(2,1)S(1)}, u32[]{:S(2)}, u32[]{:S(2)}) collective-permute-start(bf16[3,832,512]{2,1,0:T(8,128)(2,1)S(1)} %shard_map.84.held), channel_id=1, source_target_pairs={{0,1},{1,0},{2,3},{3,2},{4,5},{5,4},{6,7},{7,6},{8,9},{9,8},{10,11... | collective-permute-start | bytes 7667720 | tf_op jit(solution)/shard_map/ppermute | solution.py:141
  4.3 0.0 copy-done
  4.3 0.0 copy-done.1
  4.3 36.3 %all_gather.3.own = bf16[256,1024]{1,0:T(8,128)(2,1)S(1)} all-gather(bf16[16,1024]{1,0:T(8,128)(2,1)S(1)} %pad_maximum_fusion), channel_id=1, replica_groups=mesh['x'=4,'y'=4,'z'=16,'c'=2] {'z'}, dimensions={0}, use_global_device_ids=true | all-gather | bytes 557056 | tf_op jit(solution)/shard_map/all_gather | solution.py:151
  40.6 0.0 collective-permute-done.away
  40.6 1.7 %shard_map.85 = bf16[16,3,16,1664]{3,2,1,0:T(8,128)(2,1)S(1)} custom-call(bf16[256,1024]{1,0:T(8,128)(2,1)S(1)} %all_gather.3.own, bf16[3,832,512]{2,1,0:T(8,128)(2,1)S(1)} %shard_map.84.held, bf16[3,832,512]{2,1,0:T(8,128)(2,1)S(1)} %collective-permute-done.away), custom_call_target="tpu_custom_call" | custom-call | flops 1073741824 | bytes 4194304 | tf_op jit(solution)/shard_map/pallas_call | solution.py:23
  42.2 33.2 %all_to_all.15.got = bf16[16,3,16,1664]{3,2,1,0:T(8,128)(2,1)S(1)} all-to-all(bf16[16,3,16,1664]{3,2,1,0:T(8,128)(2,1)S(1)} %shard_map.85), channel_id=1, replica_groups={{0,32,64,96,224,192,160,288,320,352,480,448,416,384,256,128},{1,33,65,9..., dimensions={0} | all-to-all | bytes 5111808 | tf_op jit(solution)/shard_map/all_to_all | solution.py:137
  75.4 0.5 shard_map.86
  75.9 28.8 %all_to_all.16.grads = bf16[16,3,16,1664]{3,2,1,0:T(8,128)(2,1)S(1)} all-to-all(bf16[16,3,16,1664]{3,2,1,0:T(8,128)(2,1)S(1)} %shard_map.86), channel_id=1, replica_groups={{0,32,64,96,224,192,160,288,320,352,480,448,416,384,256,128},{1,33,65,9..., dimensions={0} | all-to-all | bytes 5111808 | tf_op jit(solution)/shard_map/all_to_all | solution.py:137
  104.7 1.7 %shard_map.87 = bf16[256,512]{1,0:T(8,128)(2,1)} custom-call(bf16[16,3,16,1664]{3,2,1,0:T(8,128)(2,1)S(1)} %all_to_all.16.grads, bf16[3,832,512]{2,1,0:T(8,128)(2,1)S(1)} %shard_map.84.held, bf16[3,832,512]{2,1,0:T(8,128)(2,1)S(1)} %collective-permute-done.away), custom_call_target="tpu_custom_call" | custom-call | flops 1073741824 | bytes 4194304 | tf_op jit(solution)/shard_map/pallas_call | solution.py:23
  106.4 8.9 %all-to-all-start.2 = ((bf16[16,16,512]{2,1,0:T(8,128)(2,1)}), bf16[16,16,512]{2,1,0:T(8,128)(2,1)S(1)}, u32[]{:S(2)}, u32[]{:S(2)}) async-start(bf16[16,16,512]{2,1,0:T(8,128)(2,1)} %bitcast.2), calls=%async_computation.2 | async-start | bytes 524288 | tf_op jit(solution)/shard_map/all_to_all | solution.py:124
  115.3 0.1 shard_map.89
  115.4 1.9 %collective-permute-start.1 = (bf16[256,3712]{1,0:T(8,128)(2,1)S(1)}, bf16[256,3712]{1,0:T(8,128)(2,1)S(1)}, u32[]{:S(2)}, u32[]{:S(2)}) collective-permute-start(bf16[256,3712]{1,0:T(8,128)(2,1)S(1)} %shard_map.89), channel_id=1, source_target_pairs={{0,1},{1,0},{2,3},{3,2},{4,5},{5,4},{6,7},{7,6},{8,9},{9,8},{10,11... | collective-permute-start | bytes 5701640 | tf_op jit(solution)/shard_map/ppermute | solution.py:141
  117.4 0.9 shard_map.88.first
  118.3 2.9 %collective-permute-done.1.got = bf16[256,3712]{1,0:T(8,128)(2,1)S(1)} collective-permute-done((bf16[256,3712]{1,0:T(8,128)(2,1)S(1)}, bf16[256,3712]{1,0:T(8,128)(2,1)S(1)}, u32[]{:S(2)}, u32[]{:S(2)}) %collective-permute-start.1) | collective-permute-done | bytes 1900576 | tf_op jit(solution)/shard_map/ppermute | solution.py:141
  121.2 1.9 %shard_map.90 = (bf16[832,512]{1,0:T(8,128)(2,1)}, bf16[832,512]{1,0:T(8,128)(2,1)}, bf16[832,512]{1,0:T(8,128)(2,1)}) custom-call(f32[3,832,512]{2,1,0:T(8,128)S(1)} %shard_map.88.first, bf16[256,3712]{1,0:T(8,128)(2,1)S(1)} %collective-permute-done.1.got), custom_call_target="tpu_custom_call" | custom-call | flops 256 | bytes 1 | tf_op jit(solution)/shard_map/pallas_call | solution.py:23
  123.1 6.7 %all-to-all-done.2 = bf16[16,16,512]{2,1,0:T(8,128)(2,1)S(1)} async-done(((bf16[16,16,512]{2,1,0:T(8,128)(2,1)}), bf16[16,16,512]{2,1,0:T(8,128)(2,1)S(1)}, u32[]{:S(2)}, u32[]{:S(2)}) %all-to-all-start.2) | async-done | bytes 262176 | tf_op jit(solution)/shard_map/all_to_all | solution.py:124
  129.8 0.6 reduce_sum.12
  (1 shorter events, 0.0 us)
Async XLA Ops:
  0.6 3.7 %copy-start = (bf16[16,512]{1,0:T(8,128)(2,1)S(1)}, bf16[16,512]{1,0:T(8,128)(2,1)}, u32[]{:S(2)}) copy-start(bf16[16,512]{1,0:T(8,128)(2,1)} %param.6) | copy-start | bytes 49156
  0.6 3.7 %copy-start.1 = (bf16[16,512]{1,0:T(8,128)(2,1)S(1)}, bf16[16,512]{1,0:T(8,128)(2,1)}, u32[]{:S(2)}) copy-start(bf16[16,512]{1,0:T(8,128)(2,1)} %param.5) | copy-start | bytes 49156
  2.4 38.2 %collective-permute-start = (bf16[3,832,512]{2,1,0:T(8,128)(2,1)S(1)}, bf16[3,832,512]{2,1,0:T(8,128)(2,1)S(1)}, u32[]{:S(2)}, u32[]{:S(2)}) collective-permute-start(bf16[3,832,512]{2,1,0:T(8,128)(2,1)S(1)} %shard_map.84.held), channel_id=1, source_target_pairs={{0,1},{1,0},{2,3},{3,2},{4,5},{5,4},{6,7},{7,6},{8,9},{9,8},{10,11... | collective-permute-start | bytes 7667720 | tf_op jit(solution)/shard_map/ppermute | solution.py:141
  106.4 23.3 %all-to-all-start.2 = ((bf16[16,16,512]{2,1,0:T(8,128)(2,1)}), bf16[16,16,512]{2,1,0:T(8,128)(2,1)S(1)}, u32[]{:S(2)}, u32[]{:S(2)}) async-start(bf16[16,16,512]{2,1,0:T(8,128)(2,1)} %bitcast.2), calls=%async_computation.2 | async-start | bytes 524288 | tf_op jit(solution)/shard_map/all_to_all | solution.py:124
  115.4 5.8 %collective-permute-start.1 = (bf16[256,3712]{1,0:T(8,128)(2,1)S(1)}, bf16[256,3712]{1,0:T(8,128)(2,1)S(1)}, u32[]{:S(2)}, u32[]{:S(2)}) collective-permute-start(bf16[256,3712]{1,0:T(8,128)(2,1)S(1)} %shard_map.89), channel_id=1, source_target_pairs={{0,1},{1,0},{2,3},{3,2},{4,5},{5,4},{6,7},{7,6},{8,9},{9,8},{10,11... | collective-permute-start | bytes 5701640 | tf_op jit(solution)/shard_map/ppermute | solution.py:141

commit v7 on v6

--- a/solution.py
+++ b/solution.py
@@ -38,8 +38,11 @@
 
 
 def load_kernel(*refs):
-    *weights, held, sems = refs
-    copies = [pltpu.make_async_copy(w, held.at[i], sems.at[i]) for i, w in enumerate(weights)]
+    *weights, tokens, out_grad, held, mine, sems = refs
+    width = tokens.shape[1]
+    pairs = [(w, held.at[i]) for i, w in enumerate(weights)]
+    pairs += [(tokens, mine.at[:, pl.ds(0, width)]), (out_grad, mine.at[:, pl.ds(width, width)])]
+    copies = [pltpu.make_async_copy(a, b, sems.at[i]) for i, (a, b) in enumerate(pairs)]
     for copy in copies:
         copy.start()
     for copy in copies:
@@ -57,14 +60,24 @@
 
 def parts_kernel(own, held, away, out):
     width, rows = held.shape[2], out.shape[2]
+    main = main_of(held.shape[1])
+
+    def store(part, p, start):
+        for r in range(out.shape[0]):
+            out[r, p, :, start : start + part.shape[1]] = part[r * rows : (r + 1) * rows]
+
+    rests = []
     for p in range(3):
         t = own[:, width:] if p == 2 else own[:, :width]
-        start = 0
-        for w in pieces(held, away, p):
-            part = mm(t, w, NT).astype(B)
-            for r in range(out.shape[0]):
-                out[r, p, :, start : start + w.shape[0]] = part[r * rows : (r + 1) * rows]
-            start += w.shape[0]
+        first, second, rest = pieces(held, away, p)
+        store(mm(t, first, NT).astype(B), p, 0)
+        store(mm(t, second, NT).astype(B), p, main)
+        rests.append(rest)
+    cut = rests[0].shape[0]
+    part = mm(own[:, :width], jnp.concatenate(rests[:2], 0), NT).astype(B)
+    store(part[:, :cut], 0, 2 * main)
+    store(part[:, cut:], 1, 2 * main)
+    store(mm(own[:, width:], rests[2], NT).astype(B), 2, 2 * main)
 
 
 def back_kernel(got, spread):
@@ -145,9 +158,13 @@
     hid, width = w_down.shape
     depth = lax.axis_size("z")
     weights = [pltpu.with_memory_space_constraint(w, pltpu.HBM) for w in (w_gate.T, w_up.T, w_down)]
-    held = call(load_kernel, ((3, hid, width), B), weights=weights, scratch=[pltpu.SemaphoreType.DMA((3,))])
+    held, mine = call(
+        load_kernel,
+        [((3, hid, width), B), ((tokens.shape[0], 2 * width), B)],
+        weights=weights + [pltpu.with_memory_space_constraint(v, pltpu.HBM) for v in (tokens, out_grad)],
+        scratch=[pltpu.SemaphoreType.DMA((5,))],
+    )
     away = swapped(held)
-    mine, held = lax.optimization_barrier((jnp.concatenate([tokens, out_grad], 1), held))
     own = lax.all_gather(mine, "z", axis=0, tiled=True)
     half = own.shape[0]
     ranks = SIDE * SIDE

time: 131 us -> 131 us (level)
  no operation moved by 1% of the time
where the time goes in v7:
time: 131 us; the launch traced here: 130 us
  blocking collectives  98.3 us (75%)
  starting transfers between devices  12.7 us (10%)
  waiting for transfers between devices  9.61 us (7%)
  Pallas kernels  8.42 us (6%)
    all_to_all x2, blocking collectives, over_rows(): lax.all_to_all(v, ALL, split_axis=0, concat_axis=0, tiled=True, axis_inde...  62 us
    all_gather x1, blocking collectives, per_device(): own = lax.all_gather(mine, 'z', axis=0, tiled=True)  36.3 us
    all_to_all x1, starting transfers between devices, spread_over(): return lax.all_to_all(x, axes, split_axis=0, concat_axis=0, tiled=True)  8.87 us
    pallas_call x7, Pallas kernels, call(): pl.pallas_call(body, out_shape=shapes, in_specs=[pl.BlockSpec(memory_spac...  8.42 us
    all_to_all x1, waiting for transfers between devices, spread_over(): return lax.all_to_all(x, axes, split_axis=0, concat_axis=0, tiled=True)  6.67 us
    ppermute x2, starting transfers between devices, swapped(): return lax.ppermute(x, 'c', SWAP)  3.84 us
    ppermute x2, waiting for transfers between devices, swapped(): return lax.ppermute(x, 'c', SWAP)  2.94 us
  transfers between devices with their start and end apart: 3, of which 2 were waited for; matrix products, arithmetic and copies ran while one was open for 0% of the time, Pallas kernels for 2%

profile of v7, /device:TPU:32, one launch (start us, length us, event | category | flops | bytes accessed | tf_op | source)
XLA Modules:
  0.0 130.3 jit_solution(9093338187648786756)
XLA Ops:
  0.6 1.7 %shard_map.84 = (bf16[3,832,512]{2,1,0:T(8,128)(2,1)S(1)}, bf16[16,1024]{1,0:T(8,128)(2,1)S(1)}) custom-call(bf16[832,512]{1,0:T(8,128)(2,1)} %bitcast.5, bf16[832,512]{1,0:T(8,128)(2,1)} %bitcast.6, bf16[832,512]{1,0:T(8,128)(2,1)} %refs_2_.1, bf16[16,512]{1,0:T(8,128)(2,1)} %refs_3_.1, bf16[16,512]{1,0:T(8,128)(2,1)} %refs_4_.1), custom_call_target="tpu_custom_call" | custom-call | flops 1073741824 | bytes 4194304 | tf_op jit(solution)/shard_map/pallas_call | solution.py:23
  2.4 1.9 %collective-permute-start = (bf16[3,832,512]{2,1,0:T(8,128)(2,1)S(1)}, bf16[3,832,512]{2,1,0:T(8,128)(2,1)S(1)}, u32[]{:S(2)}, u32[]{:S(2)}) collective-permute-start(bf16[3,832,512]{2,1,0:T(8,128)(2,1)S(1)} %get-tuple-element.17.held), channel_id=1, source_target_pairs={{0,1},{1,0},{2,3},{3,2},{4,5},{5,4},{6,7},{7,6},{8,9},{9,8},{10,11... | collective-permute-start | bytes 7667720 | tf_op jit(solution)/shard_map/ppermute | solution.py:154
  4.3 36.3 %all_gather.3.own = bf16[256,1024]{1,0:T(8,128)(2,1)S(1)} all-gather(bf16[16,1024]{1,0:T(8,128)(2,1)S(1)} %get-tuple-element.16), channel_id=1, replica_groups=mesh['x'=4,'y'=4,'z'=16,'c'=2] {'z'}, dimensions={0}, use_global_device_ids=true | all-gather | bytes 557056 | tf_op jit(solution)/shard_map/all_gather | solution.py:168
  40.5 0.0 collective-permute-done.away
  40.5 1.6 %shard_map.85 = bf16[16,3,16,1664]{3,2,1,0:T(8,128)(2,1)S(1)} custom-call(bf16[256,1024]{1,0:T(8,128)(2,1)S(1)} %all_gather.3.own, bf16[3,832,512]{2,1,0:T(8,128)(2,1)S(1)} %get-tuple-element.17.held, bf16[3,832,512]{2,1,0:T(8,128)(2,1)S(1)} %collective-permute-done.away), custom_call_target="tpu_custom_call" | custom-call | flops 1073741824 | bytes 4194304 | tf_op jit(solution)/shard_map/pallas_call | solution.py:23
  42.1 33.2 %all_to_all.15.got = bf16[16,3,16,1664]{3,2,1,0:T(8,128)(2,1)S(1)} all-to-all(bf16[16,3,16,1664]{3,2,1,0:T(8,128)(2,1)S(1)} %shard_map.85), channel_id=1, replica_groups={{0,32,64,96,224,192,160,288,320,352,480,448,416,384,256,128},{1,33,65,9..., dimensions={0} | all-to-all | bytes 5111808 | tf_op jit(solution)/shard_map/all_to_all | solution.py:150
  75.3 0.5 shard_map.86
  75.8 28.8 %all_to_all.16.grads = bf16[16,3,16,1664]{3,2,1,0:T(8,128)(2,1)S(1)} all-to-all(bf16[16,3,16,1664]{3,2,1,0:T(8,128)(2,1)S(1)} %shard_map.86), channel_id=1, replica_groups={{0,32,64,96,224,192,160,288,320,352,480,448,416,384,256,128},{1,33,65,9..., dimensions={0} | all-to-all | bytes 5111808 | tf_op jit(solution)/shard_map/all_to_all | solution.py:150
  104.6 1.7 %shard_map.87 = bf16[256,512]{1,0:T(8,128)(2,1)} custom-call(bf16[16,3,16,1664]{3,2,1,0:T(8,128)(2,1)S(1)} %all_to_all.16.grads, bf16[3,832,512]{2,1,0:T(8,128)(2,1)S(1)} %get-tuple-element.17.held, bf16[3,832,512]{2,1,0:T(8,128)(2,1)S(1)} %collective-permute-done.away), custom_call_target="tpu_custom_call" | custom-call | flops 1073741824 | bytes 4194304 | tf_op jit(solution)/shard_map/pallas_call | solution.py:23
  106.3 8.9 %all-to-all-start.2 = ((bf16[16,16,512]{2,1,0:T(8,128)(2,1)}), bf16[16,16,512]{2,1,0:T(8,128)(2,1)S(1)}, u32[]{:S(2)}, u32[]{:S(2)}) async-start(bf16[16,16,512]{2,1,0:T(8,128)(2,1)} %bitcast.2), calls=%async_computation.2 | async-start | bytes 524288 | tf_op jit(solution)/shard_map/all_to_all | solution.py:137
  115.2 0.1 shard_map.89
  115.3 1.9 %collective-permute-start.1 = (bf16[256,3712]{1,0:T(8,128)(2,1)S(1)}, bf16[256,3712]{1,0:T(8,128)(2,1)S(1)}, u32[]{:S(2)}, u32[]{:S(2)}) collective-permute-start(bf16[256,3712]{1,0:T(8,128)(2,1)S(1)} %shard_map.89), channel_id=1, source_target_pairs={{0,1},{1,0},{2,3},{3,2},{4,5},{5,4},{6,7},{7,6},{8,9},{9,8},{10,11... | collective-permute-start | bytes 5701640 | tf_op jit(solution)/shard_map/ppermute | solution.py:154
  117.3 0.9 shard_map.88.first
  118.2 2.9 %collective-permute-done.1.got = bf16[256,3712]{1,0:T(8,128)(2,1)S(1)} collective-permute-done((bf16[256,3712]{1,0:T(8,128)(2,1)S(1)}, bf16[256,3712]{1,0:T(8,128)(2,1)S(1)}, u32[]{:S(2)}, u32[]{:S(2)}) %collective-permute-start.1) | collective-permute-done | bytes 1900576 | tf_op jit(solution)/shard_map/ppermute | solution.py:154
  121.1 1.9 %shard_map.90 = (bf16[832,512]{1,0:T(8,128)(2,1)}, bf16[832,512]{1,0:T(8,128)(2,1)}, bf16[832,512]{1,0:T(8,128)(2,1)}) custom-call(f32[3,832,512]{2,1,0:T(8,128)S(1)} %shard_map.88.first, bf16[256,3712]{1,0:T(8,128)(2,1)S(1)} %collective-permute-done.1.got), custom_call_target="tpu_custom_call" | custom-call | flops 256 | bytes 1 | tf_op jit(solution)/shard_map/pallas_call | solution.py:23
  123.0 6.7 %all-to-all-done.2 = bf16[16,16,512]{2,1,0:T(8,128)(2,1)S(1)} async-done(((bf16[16,16,512]{2,1,0:T(8,128)(2,1)}), bf16[16,16,512]{2,1,0:T(8,128)(2,1)S(1)}, u32[]{:S(2)}, u32[]{:S(2)}) %all-to-all-start.2) | async-done | bytes 262176 | tf_op jit(solution)/shard_map/all_to_all | solution.py:137
  129.7 0.6 reduce_sum.12
Async XLA Ops:
  2.4 38.2 %collective-permute-start = (bf16[3,832,512]{2,1,0:T(8,128)(2,1)S(1)}, bf16[3,832,512]{2,1,0:T(8,128)(2,1)S(1)}, u32[]{:S(2)}, u32[]{:S(2)}) collective-permute-start(bf16[3,832,512]{2,1,0:T(8,128)(2,1)S(1)} %get-tuple-element.17.held), channel_id=1, source_target_pairs={{0,1},{1,0},{2,3},{3,2},{4,5},{5,4},{6,7},{7,6},{8,9},{9,8},{10,11... | collective-permute-start | bytes 7667720 | tf_op jit(solution)/shard_map/ppermute | solution.py:154
  106.3 23.3 %all-to-all-start.2 = ((bf16[16,16,512]{2,1,0:T(8,128)(2,1)}), bf16[16,16,512]{2,1,0:T(8,128)(2,1)S(1)}, u32[]{:S(2)}, u32[]{:S(2)}) async-start(bf16[16,16,512]{2,1,0:T(8,128)(2,1)} %bitcast.2), calls=%async_computation.2 | async-start | bytes 524288 | tf_op jit(solution)/shard_map/all_to_all | solution.py:137
  115.3 5.8 %collective-permute-start.1 = (bf16[256,3712]{1,0:T(8,128)(2,1)S(1)}, bf16[256,3712]{1,0:T(8,128)(2,1)S(1)}, u32[]{:S(2)}, u32[]{:S(2)}) collective-permute-start(bf16[256,3712]{1,0:T(8,128)(2,1)S(1)} %shard_map.89), channel_id=1, source_target_pairs={{0,1},{1,0},{2,3},{3,2},{4,5},{5,4},{6,7},{7,6},{8,9},{9,8},{10,11... | collective-permute-start | bytes 5701640 | tf_op jit(solution)/shard_map/ppermute | solution.py:154

commit v8 on v7

--- a/solution.py
+++ b/solution.py
@@ -38,11 +38,8 @@
 
 
 def load_kernel(*refs):
-    *weights, tokens, out_grad, held, mine, sems = refs
-    width = tokens.shape[1]
-    pairs = [(w, held.at[i]) for i, w in enumerate(weights)]
-    pairs += [(tokens, mine.at[:, pl.ds(0, width)]), (out_grad, mine.at[:, pl.ds(width, width)])]
-    copies = [pltpu.make_async_copy(a, b, sems.at[i]) for i, (a, b) in enumerate(pairs)]
+    *weights, held, sems = refs
+    copies = [pltpu.make_async_copy(w, held.at[i], sems.at[i]) for i, w in enumerate(weights)]
     for copy in copies:
         copy.start()
     for copy in copies:
@@ -143,7 +140,7 @@
 
 def rows_of(shape):
     ids = np.arange(int(np.prod(shape))).reshape(shape)
-    return [[int(ids[x, y, z, c]) for x, y in PATH] for z in range(shape[2]) for c in range(2)]
+    return [[int(ids[x, y, z, c]) for x, y in (PATH, PATH[::-1])[c]] for z in range(shape[2]) for c in range(2)]
 
 
 def over_rows(v, shape):
@@ -158,13 +155,9 @@
     hid, width = w_down.shape
     depth = lax.axis_size("z")
     weights = [pltpu.with_memory_space_constraint(w, pltpu.HBM) for w in (w_gate.T, w_up.T, w_down)]
-    held, mine = call(
-        load_kernel,
-        [((3, hid, width), B), ((tokens.shape[0], 2 * width), B)],
-        weights=weights + [pltpu.with_memory_space_constraint(v, pltpu.HBM) for v in (tokens, out_grad)],
-        scratch=[pltpu.SemaphoreType.DMA((5,))],
-    )
+    held = call(load_kernel, ((3, hid, width), B), weights=weights, scratch=[pltpu.SemaphoreType.DMA((3,))])
     away = swapped(held)
+    mine, held = lax.optimization_barrier((jnp.concatenate([tokens, out_grad], 1), held))
     own = lax.all_gather(mine, "z", axis=0, tiled=True)
     half = own.shape[0]
     ranks = SIDE * SIDE

time: 131 us -> 130 us (level)
  no operation moved by 1% of the time
where the time goes in v8:
time: 130 us
  blocking collectives  97.6 us (75%)
  starting transfers between devices  12.7 us (10%)
  waiting for transfers between devices  9.75 us (8%)
  Pallas kernels  8.41 us (6%)
    all_to_all x2, blocking collectives, over_rows(): lax.all_to_all(v, ALL, split_axis=0, concat_axis=0, tiled=True, axis_inde...  61.3 us
    all_gather x1, blocking collectives, per_device(): own = lax.all_gather(mine, 'z', axis=0, tiled=True)  36.3 us
    all_to_all x1, starting transfers between devices, spread_over(): return lax.all_to_all(x, axes, split_axis=0, concat_axis=0, tiled=True)  8.87 us
    pallas_call x7, Pallas kernels, call(): pl.pallas_call(body, out_shape=shapes, in_specs=[pl.BlockSpec(memory_spac...  8.41 us
    all_to_all x1, waiting for transfers between devices, spread_over(): return lax.all_to_all(x, axes, split_axis=0, concat_axis=0, tiled=True)  6.82 us
    ppermute x2, starting transfers between devices, swapped(): return lax.ppermute(x, 'c', SWAP)  3.84 us
    ppermute x2, waiting for transfers between devices, swapped(): return lax.ppermute(x, 'c', SWAP)  2.94 us
  transfers between devices with their start and end apart: 3, of which 2 were waited for; matrix products, arithmetic and copies ran while one was open for 0% of the time, Pallas kernels for 2%

profile of v8, /device:TPU:32, one launch (start us, length us, event | category | flops | bytes accessed | tf_op | source)
XLA Modules:
  0.0 129.8 jit_solution(14076792760665976110)
XLA Ops:
  0.6 0.0 copy-start
  0.6 0.0 copy-start.1
  0.7 1.7 %shard_map.84.held = bf16[3,832,512]{2,1,0:T(8,128)(2,1)S(1)} custom-call(bf16[832,512]{1,0:T(8,128)(2,1)} %bitcast.5, bf16[832,512]{1,0:T(8,128)(2,1)} %bitcast.6, bf16[832,512]{1,0:T(8,128)(2,1)} %refs_2_.1), custom_call_target="tpu_custom_call" | custom-call | flops 1073741824 | bytes 4194304 | tf_op jit(solution)/shard_map/pallas_call | solution.py:23
  2.4 1.9 %collective-permute-start = (bf16[3,832,512]{2,1,0:T(8,128)(2,1)S(1)}, bf16[3,832,512]{2,1,0:T(8,128)(2,1)S(1)}, u32[]{:S(2)}, u32[]{:S(2)}) collective-permute-start(bf16[3,832,512]{2,1,0:T(8,128)(2,1)S(1)} %shard_map.84.held), channel_id=1, source_target_pairs={{0,1},{1,0},{2,3},{3,2},{4,5},{5,4},{6,7},{7,6},{8,9},{9,8},{10,11... | collective-permute-start | bytes 7667720 | tf_op jit(solution)/shard_map/ppermute | solution.py:151
  4.3 0.0 copy-done
  4.3 0.0 copy-done.1
  4.3 36.3 %all_gather.3.own = bf16[256,1024]{1,0:T(8,128)(2,1)S(1)} all-gather(bf16[16,1024]{1,0:T(8,128)(2,1)S(1)} %pad_maximum_fusion), channel_id=1, replica_groups=mesh['x'=4,'y'=4,'z'=16,'c'=2] {'z'}, dimensions={0}, use_global_device_ids=true | all-gather | bytes 557056 | tf_op jit(solution)/shard_map/all_gather | solution.py:161
  40.6 0.0 collective-permute-done.away
  40.6 1.6 %shard_map.85 = bf16[16,3,16,1664]{3,2,1,0:T(8,128)(2,1)S(1)} custom-call(bf16[256,1024]{1,0:T(8,128)(2,1)S(1)} %all_gather.3.own, bf16[3,832,512]{2,1,0:T(8,128)(2,1)S(1)} %shard_map.84.held, bf16[3,832,512]{2,1,0:T(8,128)(2,1)S(1)} %collective-permute-done.away), custom_call_target="tpu_custom_call" | custom-call | flops 1073741824 | bytes 4194304 | tf_op jit(solution)/shard_map/pallas_call | solution.py:23
  42.1 32.6 %all_to_all.15.got = bf16[16,3,16,1664]{3,2,1,0:T(8,128)(2,1)S(1)} all-to-all(bf16[16,3,16,1664]{3,2,1,0:T(8,128)(2,1)S(1)} %shard_map.85), channel_id=1, replica_groups={{0,32,64,96,224,192,160,288,320,352,480,448,416,384,256,128},{129,257,3..., dimensions={0} | all-to-all | bytes 5111808 | tf_op jit(solution)/shard_map/all_to_all | solution.py:147
  74.8 0.5 shard_map.86
  75.2 28.7 %all_to_all.16.grads = bf16[16,3,16,1664]{3,2,1,0:T(8,128)(2,1)S(1)} all-to-all(bf16[16,3,16,1664]{3,2,1,0:T(8,128)(2,1)S(1)} %shard_map.86), channel_id=1, replica_groups={{0,32,64,96,224,192,160,288,320,352,480,448,416,384,256,128},{129,257,3..., dimensions={0} | all-to-all | bytes 5111808 | tf_op jit(solution)/shard_map/all_to_all | solution.py:147
  103.9 1.7 %shard_map.87 = bf16[256,512]{1,0:T(8,128)(2,1)} custom-call(bf16[16,3,16,1664]{3,2,1,0:T(8,128)(2,1)S(1)} %all_to_all.16.grads, bf16[3,832,512]{2,1,0:T(8,128)(2,1)S(1)} %shard_map.84.held, bf16[3,832,512]{2,1,0:T(8,128)(2,1)S(1)} %collective-permute-done.away), custom_call_target="tpu_custom_call" | custom-call | flops 1073741824 | bytes 4194304 | tf_op jit(solution)/shard_map/pallas_call | solution.py:23
  105.7 8.9 %all-to-all-start.2 = ((bf16[16,16,512]{2,1,0:T(8,128)(2,1)}), bf16[16,16,512]{2,1,0:T(8,128)(2,1)S(1)}, u32[]{:S(2)}, u32[]{:S(2)}) async-start(bf16[16,16,512]{2,1,0:T(8,128)(2,1)} %bitcast.2), calls=%async_computation.2 | async-start | bytes 524288 | tf_op jit(solution)/shard_map/all_to_all | solution.py:134
  114.5 0.1 shard_map.89
  114.7 1.9 %collective-permute-start.1 = (bf16[256,3712]{1,0:T(8,128)(2,1)S(1)}, bf16[256,3712]{1,0:T(8,128)(2,1)S(1)}, u32[]{:S(2)}, u32[]{:S(2)}) collective-permute-start(bf16[256,3712]{1,0:T(8,128)(2,1)S(1)} %shard_map.89), channel_id=1, source_target_pairs={{0,1},{1,0},{2,3},{3,2},{4,5},{5,4},{6,7},{7,6},{8,9},{9,8},{10,11... | collective-permute-start | bytes 5701640 | tf_op jit(solution)/shard_map/ppermute | solution.py:151
  116.6 0.9 shard_map.88.first
  117.5 2.9 %collective-permute-done.1.got = bf16[256,3712]{1,0:T(8,128)(2,1)S(1)} collective-permute-done((bf16[256,3712]{1,0:T(8,128)(2,1)S(1)}, bf16[256,3712]{1,0:T(8,128)(2,1)S(1)}, u32[]{:S(2)}, u32[]{:S(2)}) %collective-permute-start.1) | collective-permute-done | bytes 1900576 | tf_op jit(solution)/shard_map/ppermute | solution.py:151
  120.5 1.9 %shard_map.90 = (bf16[832,512]{1,0:T(8,128)(2,1)}, bf16[832,512]{1,0:T(8,128)(2,1)}, bf16[832,512]{1,0:T(8,128)(2,1)}) custom-call(f32[3,832,512]{2,1,0:T(8,128)S(1)} %shard_map.88.first, bf16[256,3712]{1,0:T(8,128)(2,1)S(1)} %collective-permute-done.1.got), custom_call_target="tpu_custom_call" | custom-call | flops 256 | bytes 1 | tf_op jit(solution)/shard_map/pallas_call | solution.py:23
  122.4 6.8 %all-to-all-done.2 = bf16[16,16,512]{2,1,0:T(8,128)(2,1)S(1)} async-done(((bf16[16,16,512]{2,1,0:T(8,128)(2,1)}), bf16[16,16,512]{2,1,0:T(8,128)(2,1)S(1)}, u32[]{:S(2)}, u32[]{:S(2)}) %all-to-all-start.2) | async-done | bytes 262176 | tf_op jit(solution)/shard_map/all_to_all | solution.py:134
  129.2 0.6 reduce_sum.12
  (1 shorter events, 0.0 us)
Async XLA Ops:
  0.6 3.7 %copy-start = (bf16[16,512]{1,0:T(8,128)(2,1)S(1)}, bf16[16,512]{1,0:T(8,128)(2,1)}, u32[]{:S(2)}) copy-start(bf16[16,512]{1,0:T(8,128)(2,1)} %param.6) | copy-start | bytes 49156
  0.6 3.7 %copy-start.1 = (bf16[16,512]{1,0:T(8,128)(2,1)S(1)}, bf16[16,512]{1,0:T(8,128)(2,1)}, u32[]{:S(2)}) copy-start(bf16[16,512]{1,0:T(8,128)(2,1)} %param.5) | copy-start | bytes 49156
  2.4 38.2 %collective-permute-start = (bf16[3,832,512]{2,1,0:T(8,128)(2,1)S(1)}, bf16[3,832,512]{2,1,0:T(8,128)(2,1)S(1)}, u32[]{:S(2)}, u32[]{:S(2)}) collective-permute-start(bf16[3,832,512]{2,1,0:T(8,128)(2,1)S(1)} %shard_map.84.held), channel_id=1, source_target_pairs={{0,1},{1,0},{2,3},{3,2},{4,5},{5,4},{6,7},{7,6},{8,9},{9,8},{10,11... | collective-permute-start | bytes 7667720 | tf_op jit(solution)/shard_map/ppermute | solution.py:151
  105.7 23.5 %all-to-all-start.2 = ((bf16[16,16,512]{2,1,0:T(8,128)(2,1)}), bf16[16,16,512]{2,1,0:T(8,128)(2,1)S(1)}, u32[]{:S(2)}, u32[]{:S(2)}) async-start(bf16[16,16,512]{2,1,0:T(8,128)(2,1)} %bitcast.2), calls=%async_computation.2 | async-start | bytes 524288 | tf_op jit(solution)/shard_map/all_to_all | solution.py:134
  114.7 5.8 %collective-permute-start.1 = (bf16[256,3712]{1,0:T(8,128)(2,1)S(1)}, bf16[256,3712]{1,0:T(8,128)(2,1)S(1)}, u32[]{:S(2)}, u32[]{:S(2)}) collective-permute-start(bf16[256,3712]{1,0:T(8,128)(2,1)S(1)} %shard_map.89), channel_id=1, source_target_pairs={{0,1},{1,0},{2,3},{3,2},{4,5},{5,4},{6,7},{7,6},{8,9},{9,8},{10,11... | collective-permute-start | bytes 5701640 | tf_op jit(solution)/shard_map/ppermute | solution.py:151
